TPU v7x, 32 devices: a whole 2x2x4 slice. The times are simulated.
32 devices in a mesh: section: 8 (over y, x, core), dp: 4 (over z).
Axes of the slice: x: 2, y: 2, z: 4, core: 2. Of those that a mesh axis runs over, the one named last changes fastest.
Arguments:
- inputs: bfloat16 [4096, 8192], P(('section', 'dp')), may hold values from -6 to 6
- hidden_grad: bfloat16 [4096, 1024], P(('section', 'dp')), may hold values from -12 to 12
- gate_pre: bfloat16 [4096, 1024], P(('section', 'dp')), may hold values from -8 to 8
- up_weight: bfloat16 [65536, 1024], P(('section', 'dp')), may hold values from -0.1875 to 0.1875
- row_state: float32 [65536], P(('section', 'dp')), may hold values from 100 to 3000
- col_state: float32 [8192], P('section'), may hold values from 100 to 3000
Outputs:
- upstream: bfloat16 [4096, 8192], P(('section', 'dp'))
- param_step: bfloat16 [65536, 1024], P(('section', 'dp'))
- row_out: float32 [65536], P(('section', 'dp'))
- col_out: float32 [8192], P('section')
All inputs are finite; a program needn't handle non-finite values.
Results may differ from a plain program's by a relative error of at most 0.0049.
Values may be sent and summed in bfloat16 or wider, within the bound.
No kernel may reach another device: no remote copies, remote signals or barrier semaphores. Data moves between devices by JAX's collectives and lax.ppermute only.
A program may use at most 128 MiB of HBM per device.

v0:
```python
import jax
import jax.numpy as jnp
from jax import lax
from jax.sharding import PartitionSpec as P

D = 8192
FF = 1024


BETA_TWO = 0.75
TINY_ADD = 1e-30


def shifted(value, axis, steps):
    count = lax.axis_size(axis)
    initial, last = (max(0, -steps), min(count, count - steps))
    return lax.ppermute(value, axis, [(source, source + steps) for source in range(initial, last)])


def local(inputs, hidden_grad, gate_pre, up_weight, row_state, col_state):
    cotangent = (
        hidden_grad.astype(jnp.float32) * jax.nn.silu(gate_pre.astype(jnp.float32))
    ).astype(jnp.bfloat16)
    gathered = lax.all_gather(cotangent, "dp", axis=0, tiled=True)
    columns = lax.all_to_all(inputs, "dp", split_axis=1, concat_axis=0, tiled=True)
    local_block = lax.dot_general(
        gathered, up_weight, (((1,), (1,)), ((), ())), preferred_element_type=jnp.float32
    ).astype(jnp.bfloat16)
    lowered = lax.all_to_all(local_block, "dp", split_axis=0, concat_axis=1, tiled=True)
    gradient = lax.dot_general(
        columns, gathered, (((0,), (0,)), ((), ())), preferred_element_type=jnp.float32
    )
    upstream = shifted(lowered, "section", -1)
    squares = gradient * gradient + TINY_ADD
    row_new = BETA_TWO * row_state + (1.0 - BETA_TWO) * jnp.mean(squares, axis=1)
    entries = float(D) * float(FF)
    col_partial, row_total = lax.psum((jnp.sum(squares, axis=0), jnp.sum(row_new)), "dp")
    col_new = BETA_TWO * col_state + (1.0 - BETA_TWO) * (col_partial / D)
    row_average = row_total / D
    second = row_new[:, None] * col_new[None, :] / row_average
    update = gradient / jnp.sqrt(second)
    grand_total = lax.psum(jnp.sum(update * update), "dp")
    root_mean = jnp.sqrt(grand_total / entries)
    step_out = (update / jnp.maximum(1.0, root_mean)).astype(jnp.bfloat16)
    return (upstream, step_out, row_new, col_new)


def solution(mesh):
    placed = (
        P(("section", "dp"), None),
        P(("section", "dp"), None),
        P(("section", "dp"), None),
        P(("section", "dp"), None),
        P(("section", "dp")),
        P("section"),
    )
    return jax.shard_map(
        local,
        mesh=mesh,
        in_specs=placed,
        out_specs=(
            P(("section", "dp"), None),
            P(("section", "dp"), None),
            P(("section", "dp")),
            P("section"),
        ),
        check_vma=False,
    )
```

profile of v0, /device:TPU:3, one launch (start us, length us, event | category | flops | bytes accessed | tf_op | source)
XLA Modules:
  0.0 180.3 jit_solution(17437607406707478870)
XLA Ops:
  7.2 4.1 %copy.15 = bf16[128,8192]{0,1:T(8,128)(2,1)} copy(bf16[128,8192]{1,0:T(8,128)(2,1)} %param.6) | data formatting | bytes 4194304 | tf_op args[0]
  11.3 4.6 %all-to-all-start.1 = ((bf16[128,4,2048]{0,2,1:T(8,128)(2,1)}), bf16[128,4,2048]{0,2,1:T(8,128)(2,1)S(1)}, u32[]{:S(2)}, u32[]{:S(2)}) async-start(bf16[128,4,2048]{0,2,1:T(8,128)(2,1)} %bitcast.26), calls=%async_computation.1 | async-start | bytes 4194304 | tf_op jit(solution)/shard_map/all_to_all | solution.py:25
  15.9 0.9 fusion.7
  16.8 0.0 all-gather.2.cloned.1.call-update
  16.8 52.8 %all-gather.2.cloned.1.call-done = bf16[512,1024]{1,0:T(8,128)(2,1)} async-done(((bf16[128,1024]{1,0:T(8,128)(2,1)}), bf16[512,1024]{1,0:T(8,128)(2,1)}) %all-gather.2.cloned.1.call-update) | async-done | bytes 1048592 | tf_op jit(solution)/shard_map/all_gather | solution.py:24
  69.6 6.3 %convolution_convert_fusion = bf16[512,2048]{1,0:T(8,128)(2,1)} fusion(bf16[512,1024]{1,0:T(8,128)(2,1)} %all-gather.2.cloned.1.call-done, bf16[2048,1024]{1,0:T(8,128)(2,1)} %param.9), kind=kOutput, calls=%fused_computation.7 | convolution fusion | flops 2148532224 | bytes 7340032 | tf_op jit(solution)/shard_map/dot_general | solution.py:26
  75.8 4.6 %all-to-all-done.1 = bf16[128,4,2048]{0,2,1:T(8,128)(2,1)S(1)} async-done(((bf16[128,4,2048]{0,2,1:T(8,128)(2,1)}), bf16[128,4,2048]{0,2,1:T(8,128)(2,1)S(1)}, u32[]{:S(2)}, u32[]{:S(2)}) %all-to-all-start.1) | async-done | bytes 2097184 | tf_op jit(solution)/shard_map/all_to_all | solution.py:25
  80.5 1.3 copy-done
  81.8 7.2 %all-to-all-start = ((bf16[4,128,2048]{2,1,0:T(8,128)(2,1)}), bf16[4,128,2048]{2,1,0:T(8,128)(2,1)S(1)}, u32[]{:S(2)}, u32[]{:S(2)}) async-start(bf16[4,128,2048]{2,1,0:T(8,128)(2,1)} %bitcast.27), calls=%async_computation | async-start | bytes 4194304 | tf_op jit(solution)/shard_map/all_to_all | solution.py:29
  89.0 4.0 %copy.16 = bf16[4,128,2048]{2,1,0:T(8,128)(2,1)} copy(bf16[4,128,2048]{1,2,0:T(8,128)(2,1)} %bitcast.25) | data formatting | bytes 4194304 | tf_op jit(solution)/shard_map/all_to_all | solution.py:25
  93.0 7.7 %fusion.1 = (f32[1024]{0:T(1024)S(1)}, f32[2048]{0:T(1024)S(1)}, f32[1024,2048]{1,0:T(8,128)}) fusion(bf16[512,1024]{1,0:T(8,128)(2,1)S(1)} %copy-done.7, bf16[512,2048]{1,0:T(8,128)(2,1)} %bitcast.28), kind=kOutput, calls=%fused_computation.5 | convolution fusion | flops 2155869184 | bytes 11546624 | tf_op jit(solution)/shard_map/dot_general | solution.py:30
  100.7 0.6 fusion.8
  101.3 27.0 %all-reduce = (f32[]{:T(128)}, f32[1024]{0:T(1024)S(1)}) all-reduce(f32[]{:T(128)} %get-tuple-element.20, f32[1024]{0:T(1024)S(1)} %get-tuple-element.16), channel_id=1, replica_groups=mesh['section'=8,'dp'=4] {'dp'}, use_global_device_ids=true, to_apply=%region_4.5 | all-reduce | flops 1025 | bytes 8200 | tf_op jit(solution)/shard_map/psum | solution.py:37
  129.0 0.0 copy-done.6
  129.0 0.0 copy-start.4
  129.0 8.1 %all-to-all-done = bf16[4,128,2048]{2,1,0:T(8,128)(2,1)S(1)} async-done(((bf16[4,128,2048]{2,1,0:T(8,128)(2,1)}), bf16[4,128,2048]{2,1,0:T(8,128)(2,1)S(1)}, u32[]{:S(2)}, u32[]{:S(2)}) %all-to-all-start) | async-done | bytes 2097184 | tf_op jit(solution)/shard_map/all_to_all | solution.py:29
  137.1 1.5 copy.18
  138.6 3.4 %collective-permute-start = (bf16[128,8192]{1,0:T(8,128)(2,1)}, bf16[128,8192]{1,0:T(8,128)(2,1)S(1)}, u32[]{:S(2)}, u32[]{:S(2)}) collective-permute-start(bf16[128,8192]{1,0:T(8,128)(2,1)} %bitcast.7), channel_id=1, source_target_pairs={{4,0},{8,4},{12,8},{16,12},{20,16},{24,20},{28,24},{5,1},{9,5},{13... | collective-permute-start | bytes 6291464 | tf_op jit(solution)/shard_map/ppermute | solution.py:17
  142.0 5.7 %multiply_reduce_fusion = f32[]{:T(128)} fusion(f32[]{:T(128)S(6)} %div.30, f32[1024]{0:T(1024)S(1)} %multiply_add_fusion.1, f32[2048]{0:T(1024)S(1)} %get-tuple-element.29, f32[1024,2048]{1,0:T(8,128)} %get-tuple-element.22), kind=kLoop, calls=%fused_computation.4 | loop fusion | flops 10485759 | bytes 8400904 | tf_op jit(solution)/shard_map/reduce_sum | solution.py:42
  147.6 11.7 %psum.23 = f32[]{:T(128)} all-reduce(f32[]{:T(128)} %multiply_reduce_fusion), channel_id=1, replica_groups=mesh['section'=8,'dp'=4] {'dp'}, use_global_device_ids=true, to_apply=%region_6.7 | all-reduce | flops 1 | bytes 8 | tf_op jit(solution)/shard_map/psum | solution.py:42
  160.1 5.7 %divide_convert_fusion = bf16[2048,1024]{0,1:T(8,128)(2,1)} fusion(f32[]{:T(128)S(6)} %max_shard_map.3, f32[]{:T(128)S(6)} %div.30, f32[1024]{0:T(1024)S(1)} %multiply_add_fusion.1, f32[2048]{0:T(1024)S(1)} %get-tuple-element.29, f32[1024,2048]{1,0:T(8,128)} %get-tuple-element.22), kind=kLoop, calls=%fused_computation.3 | loop fusion | flops 10485760 | bytes 12595208 | tf_op jit(solution)/shard_map/convert_element_type | solution.py:44
  165.7 6.4 %copy.17 = bf16[2048,1024]{1,0:T(8,128)(2,1)} copy(bf16[2048,1024]{0,1:T(8,128)(2,1)} %divide_convert_fusion) | data formatting | bytes 8388608
  172.1 0.0 collective-permute-done
  172.1 1.3 copy.20
  (15 shorter events, 0.0 us)
Async XLA Ops:
  7.2 8.7 %copy-start.2 = (bf16[128,1024]{1,0:T(8,128)(2,1)S(1)}, bf16[128,1024]{1,0:T(8,128)(2,1)}, u32[]{:S(2)}) copy-start(bf16[128,1024]{1,0:T(8,128)(2,1)} %param.7) | copy-start | bytes 786436
  7.2 8.7 %copy-start.1 = (bf16[128,1024]{1,0:T(8,128)(2,1)S(1)}, bf16[128,1024]{1,0:T(8,128)(2,1)}, u32[]{:S(2)}) copy-start(bf16[128,1024]{1,0:T(8,128)(2,1)} %param.8) | copy-start | bytes 786436
  11.3 69.1 %all-to-all-start.1 = ((bf16[128,4,2048]{0,2,1:T(8,128)(2,1)}), bf16[128,4,2048]{0,2,1:T(8,128)(2,1)S(1)}, u32[]{:S(2)}, u32[]{:S(2)}) async-start(bf16[128,4,2048]{0,2,1:T(8,128)(2,1)} %bitcast.26), calls=%async_computation.1 | async-start | bytes 4194304 | tf_op jit(solution)/shard_map/all_to_all | solution.py:25
  15.9 53.7 %all-gather.2.cloned.1.call-start = ((), (), s32[]{:S(2)}) async-start(), calls=%async_computation.2 | async-start | bytes 1310720 | tf_op jit(solution)/shard_map/all_gather | solution.py:24
  69.6 23.5 %copy-start.7 = (bf16[512,1024]{1,0:T(8,128)(2,1)S(1)}, bf16[512,1024]{1,0:T(8,128)(2,1)}, u32[]{:S(2)}) copy-start(bf16[512,1024]{1,0:T(8,128)(2,1)} %all-gather.2.cloned.1.call-done) | copy-start | bytes 3145732
  80.5 1.3 copy-start
  81.8 55.3 %all-to-all-start = ((bf16[4,128,2048]{2,1,0:T(8,128)(2,1)}), bf16[4,128,2048]{2,1,0:T(8,128)(2,1)S(1)}, u32[]{:S(2)}, u32[]{:S(2)}) async-start(bf16[4,128,2048]{2,1,0:T(8,128)(2,1)} %bitcast.27), calls=%async_computation | async-start | bytes 4194304 | tf_op jit(solution)/shard_map/all_to_all | solution.py:29
  93.0 7.7 %copy-start.5 = (f32[2048]{0:T(1024)S(1)}, f32[2048]{0:T(1024)}, u32[]{:S(2)}) copy-start(f32[2048]{0:T(1024)} %param.10) | copy-start | bytes 24580
  93.0 36.0 %copy-start.6 = (f32[1024]{0:T(1024)S(1)}, f32[1024]{0:T(1024)}, u32[]{:S(2)}) copy-start(f32[1024]{0:T(1024)} %param.11) | copy-start | bytes 12292
  101.3 64.4 %copy-start.3 = (f32[2048]{0:T(1024)}, f32[2048]{0:T(1024)S(1)}, u32[]{:S(2)}) copy-start(f32[2048]{0:T(1024)S(1)} %get-tuple-element.29) | copy-start | bytes 24580
  129.0 36.7 %copy-start.4 = (f32[1024]{0:T(1024)}, f32[1024]{0:T(1024)S(1)}, u32[]{:S(2)}) copy-start(f32[1024]{0:T(1024)S(1)} %multiply_add_fusion.1) | copy-start | bytes 12292
  138.6 33.6 %collective-permute-start = (bf16[128,8192]{1,0:T(8,128)(2,1)}, bf16[128,8192]{1,0:T(8,128)(2,1)S(1)}, u32[]{:S(2)}, u32[]{:S(2)}) collective-permute-start(bf16[128,8192]{1,0:T(8,128)(2,1)} %bitcast.7), channel_id=1, source_target_pairs={{4,0},{8,4},{12,8},{16,12},{20,16},{24,20},{28,24},{5,1},{9,5},{13... | collective-permute-start | bytes 6291464 | tf_op jit(solution)/shard_map/ppermute | solution.py:17
Sparse Core Ops, SparseCore 0:
  18.9 50.6 all-gather.1
where the time goes:
time: 183 us; the launch traced here: 180 us
  waiting for transfers between devices  65.5 us (36%)
  blocking collectives  38.7 us (21%)
  local copies, waits for them, and re-layouts  18.6 us (10%)
  between operations  15.4 us (8%)
  starting transfers between devices  15.2 us (8%)
  matrix products  14 us (8%)
  other arithmetic  12.8 us (7%)
    all_gather x1, waiting for transfers between devices, local(): gathered = lax.all_gather(cotangent, 'dp', axis=0, tiled=True)  52.8 us
    psum x1, blocking collectives, local(): lax.psum((jnp.sum(squares, axis=0), jnp.sum(row_new)), 'dp')  27 us
    unnamed x19, local copies, waits for them, and re-layouts  13.2 us
    psum x1, blocking collectives, local(): grand_total = lax.psum(jnp.sum(update * update), 'dp')  11.7 us
    all_to_all x1, waiting for transfers between devices, local(): lax.all_to_all(local_block, 'dp', split_axis=0, concat_axis=1, tiled=True)  8.1 us
    dot_general x1, matrix products, local(): lax.dot_general(columns, gathered, (((0,), (0,)), ((), ())), preferred_el...  7.7 us
    all_to_all x1, starting transfers between devices, local(): lax.all_to_all(local_block, 'dp', split_axis=0, concat_axis=1, tiled=True)  7.24 us
    dot_general x1, matrix products, local(): lax.dot_general(gathered, up_weight, (((1,), (1,)), ((), ())), preferred_...  6.28 us
  transfers between devices with their start and end apart: 4, of which 3 were waited for; matrix products, arithmetic and copies ran while one was open for 21% of the time, Pallas kernels for 0%

commit v1 on v0

v1 whole, which is shorter than its diff:
```python
import functools

import jax
import jax.numpy as jnp
from jax import lax
from jax.experimental import pallas as pl
from jax.experimental.pallas import tpu as pltpu
from jax.sharding import PartitionSpec as P

BETA_TWO = 0.75
TINY_ADD = 1e-30
SECTION, DP = "section", "dp"


def after(value, *others):
    return lax.optimization_barrier((value, *others))[0]


def ring(value, steps):
    count = lax.axis_size(DP)
    return lax.ppermute(value, DP, [(i, (i + steps) % count) for i in range(count)])


def hop(value, origin, steps):
    count = lax.axis_size(DP)
    if steps > 0:
        pairs = [(i, i + 1) for i in range(origin, count - 1)]
    else:
        pairs = [(i, i - 1) for i in range(1, count - origin)]
    return lax.ppermute(value, DP, pairs)


def hand_over(value, steps):
    count, sections = lax.axis_size(DP), lax.axis_size(SECTION)
    pairs = [
        (s * count + i, (s - 1) * count + (i + steps) % count)
        for s in range(1, sections)
        for i in range(count)
    ]
    return lax.ppermute(value, (SECTION, DP), pairs)


def gradient_kernel(parts, entries_per_row, *refs):
    xs, cs = refs[:parts], refs[parts : 2 * parts]
    state_ref, grad_ref, row_ref, col_ref, weighted_ref = refs[2 * parts :]
    step = pl.program_id(0)
    x = jnp.concatenate([r[...] for r in xs], axis=0)
    c = jnp.concatenate([r[...] for r in cs], axis=0)
    grad = lax.dot_general(
        x, c, (((0,), (0,)), ((), ())), preferred_element_type=jnp.float32
    )
    grad_ref[...] = grad
    plain = grad * grad
    squares = plain + TINY_ADD
    row = BETA_TWO * state_ref[...] + (1.0 - BETA_TWO) * (
        jnp.sum(squares, axis=1, keepdims=True) / entries_per_row
    )
    row_ref[...] = row

    @pl.when(step == 0)
    def _():
        col_ref[...] = jnp.zeros_like(col_ref)
        weighted_ref[...] = jnp.zeros_like(weighted_ref)

    col_ref[...] += jnp.sum(squares, axis=0, keepdims=True)
    weighted_ref[...] += jnp.sum(plain / row, axis=0, keepdims=True)


def gradient_call(xs, cs, row_state, block=256):
    parts = len(xs)
    tokens, rows = xs[0].shape
    units = cs[0].shape[1]
    block = min(block, rows)
    return pl.pallas_call(
        functools.partial(gradient_kernel, parts, float(units)),
        grid=(rows // block,),
        in_specs=[pl.BlockSpec((tokens, block), lambda i: (0, i))] * parts
        + [pl.BlockSpec((tokens, units), lambda i: (0, 0))] * parts
        + [pl.BlockSpec((block, 1), lambda i: (i, 0))],
        out_specs=[
            pl.BlockSpec((block, units), lambda i: (i, 0)),
            pl.BlockSpec((block, 1), lambda i: (i, 0)),
            pl.BlockSpec((1, units), lambda i: (0, 0)),
            pl.BlockSpec((1, units), lambda i: (0, 0)),
        ],
        out_shape=[
            jax.ShapeDtypeStruct((rows, units), jnp.float32),
            jax.ShapeDtypeStruct((rows, 1), jnp.float32),
            jax.ShapeDtypeStruct((1, units), jnp.float32),
            jax.ShapeDtypeStruct((1, units), jnp.float32),
        ],
        compiler_params=pltpu.CompilerParams(vmem_limit_bytes=32 * 1024 * 1024),
        cost_estimate=pl.CostEstimate(
            flops=2 * parts * tokens * rows * units,
            bytes_accessed=parts * tokens * (rows + units) * 2 + rows * units * 4,
            transcendentals=0,
        ),
        name="gradient_and_sums",
    )(*xs, *cs, row_state[:, None])


def local(inputs, hidden_grad, gate_pre, up_weight, row_state, col_state):
    count = lax.axis_size(DP)
    me = lax.axis_index(DP)
    tokens, width = inputs.shape
    rows, units = up_weight.shape

    def columns_of(owner):
        return lax.dynamic_slice_in_dim(inputs, owner * rows, rows, axis=1)

    def lowered(cot):
        return lax.dot_general(
            cot, up_weight, (((1,), (1,)), ((), ())), preferred_element_type=jnp.float32
        ).astype(jnp.bfloat16)

    cotangent = (
        hidden_grad.astype(jnp.float32) * jax.nn.silu(gate_pre.astype(jnp.float32))
    ).astype(jnp.bfloat16)

    ahead, behind = {0: cotangent}, {0: cotangent}
    for j in range(1, count):
        ahead[j] = hop(ahead[j - 1], j - 1, 1)
        behind[j] = hop(behind[j - 1], j - 1, -1)
    cots = [cotangent] + [
        jnp.where(me >= k, ahead[k], behind[count - k]) for k in range(1, count)
    ]
    xs = [columns_of(me)] + [
        ring(columns_of(lax.rem(me + k, count)), k) for k in range(1, count)
    ]

    grad, row_new, col_sum, weighted = gradient_call(xs, cots, row_state)
    row_new = row_new[:, 0]
    sums = jnp.concatenate(
        [col_sum[0], weighted[0], jnp.full((units,), jnp.sum(row_new))]
    ).reshape(-1, 128)
    pieces = jnp.stack([sums] + [ring(sums, k) for k in range(1, count)])
    total = jnp.zeros_like(sums)
    for owner in range(count):
        total = total + lax.dynamic_index_in_dim(
            pieces, lax.rem(me - owner + count, count), 0, keepdims=False
        )
    total = total.reshape(3, units)
    row_average = total[2, 0] / width
    col_new = BETA_TWO * col_state + (1.0 - BETA_TWO) * (total[0] / width)
    grand_total = row_average * jnp.sum(total[1] / col_new)
    root_mean = jnp.sqrt(grand_total / (float(width) * float(units)))
    col_factor = lax.rsqrt(col_new) * (jnp.sqrt(row_average) / jnp.maximum(1.0, root_mean))
    step_out = (grad * (lax.rsqrt(row_new)[:, None] * col_factor[None, :])).astype(jnp.bfloat16)

    upstream = jnp.zeros((tokens, width), jnp.bfloat16)
    for k in range(count):
        part = hand_over(lowered(cots[(count - k) % count]), k)
        owner = lax.rem(me - k + count, count)
        upstream = lax.dynamic_update_slice_in_dim(upstream, part, owner * rows, axis=1)
    return (upstream, step_out, row_new, col_new)


def solution(mesh):
    blocks = P((SECTION, DP), None)
    vector = P((SECTION, DP))
    return jax.shard_map(
        local,
        mesh=mesh,
        in_specs=(blocks, blocks, blocks, blocks, vector, P(SECTION)),
        out_specs=(blocks, blocks, vector, P(SECTION)),
        check_vma=False,
    )
```

time: 183 us -> 132 us (0.72); the launches traced: 180 us -> 131 us
  blocking collectives: 38.7 us -> 0 us
  starting transfers between devices: 15.2 us -> 35.9 us
  between operations: 15.4 us -> 2.46 us
  local copies, waits for them, and re-layouts: 18.6 us -> 7.84 us
  Pallas kernels: 0 us -> 6.4 us
  waiting for transfers between devices: 65.5 us -> 59.6 us
  matrix products: 14 us -> 9.04 us
  other arithmetic: 12.8 us -> 9.96 us
    ppermute x1 -> x16, waiting for transfers between devices: 0.01 us -> 59.6 us  [the longest x6 44.1 us: hop(): return lax.ppermute(value, DP, pairs)]
    all_gather x1 -> x0, waiting for transfers between devices: 52.8 us -> none  [local(): gathered = lax.all_gather(cotangent, 'dp', axis=0, tiled=True)]
    psum x2 -> x0, blocking collectives: 38.7 us -> none  [the longest x1 27 us: local(): lax.psum((jnp.sum(squares, axis=0), jnp.sum(row_new)), 'dp')]
    ppermute x1 -> x16, starting transfers between devices: 3.4 us -> 35.9 us  [the longest x6 14 us: ring(): lax.ppermute(value, DP, [(i, (i + steps) % count) for i in range(count)])]
    all_to_all x2 -> x0, waiting for transfers between devices: 12.7 us -> none  [the longest x1 8.1 us: local(): lax.all_to_all(local_block, 'dp', split_axis=0, concat_axis=1, tiled=True)]
    unnamed x19 -> x16, local copies, waits for them, and re-layouts: 13.2 us -> 1.35 us
    all_to_all x2 -> x0, starting transfers between devices: 11.8 us -> none  [the longest x1 7.24 us: local(): lax.all_to_all(local_block, 'dp', split_axis=0, concat_axis=1, tiled=True)]
    pallas_call x0 -> x1, Pallas kernels: none -> 6.4 us  [gradient_call(): pl.pallas_call(functools.partial(gradient_kernel, parts, float(units)), g...]
  transfers between devices with their start and end apart: 4 -> 16, of which waited for: 3 -> 4; matrix products, arithmetic and copies ran while one was open for 21% -> 18% of each run, Pallas kernels for 0% -> 5%
where the time goes in v1:
time: 132 us; the launch traced here: 131 us
  waiting for transfers between devices  59.6 us (45%)
  starting transfers between devices  35.9 us (27%)
  other arithmetic  9.96 us (8%)
  matrix products  9.04 us (7%)
  local copies, waits for them, and re-layouts  7.84 us (6%)
  Pallas kernels  6.4 us (5%)
  between operations  2.46 us (2%)
    ppermute x6, waiting for transfers between devices, hop(): return lax.ppermute(value, DP, pairs)  44.1 us
    ppermute x4, waiting for transfers between devices, hand_over(): return lax.ppermute(value, (SECTION, DP), pairs)  15.5 us
    ppermute x6, starting transfers between devices, ring(): lax.ppermute(value, DP, [(i, (i + steps) % count) for i in range(count)])  14 us
    ppermute x4, starting transfers between devices, hand_over(): return lax.ppermute(value, (SECTION, DP), pairs)  12.6 us
    ppermute x6, starting transfers between devices, hop(): return lax.ppermute(value, DP, pairs)  9.39 us
    dot_general x4, matrix products, lowered(): lax.dot_general(cot, up_weight, (((1,), (1,)), ((), ())), preferred_eleme...  9.04 us
    pallas_call x1, Pallas kernels, gradient_call(): pl.pallas_call(functools.partial(gradient_kernel, parts, float(units)), g...  6.4 us
    convert_element_type x1, other arithmetic, local(): (grad * (lax.rsqrt(row_new)[:, None] * col_factor[None, :])).astype(jnp.b...  5.34 us
  transfers between devices with their start and end apart: 16, of which 4 were waited for; matrix products, arithmetic and copies ran while one was open for 18% of the time, Pallas kernels for 5%

profile of v1, /device:TPU:3, one launch (start us, length us, event | category | flops | bytes accessed | tf_op | source)
XLA Modules:
  0.0 131.2 jit_solution(9140264323775957219)
XLA Ops:
  1.8 3.9 %collective-permute-start.1 = (bf16[128,1024]{1,0:T(8,128)(2,1)S(1)}, bf16[128,1024]{1,0:T(8,128)(2,1)}, u32[]{:S(2)}, u32[]{:S(2)}) collective-permute-start(bf16[128,1024]{1,0:T(8,128)(2,1)S(1)} %fusion.4.refs_4_), channel_id=1, source_target_pairs={{0,1},{1,2},{2,3},{4,5},{5,6},{6,7},{8,9},{9,10},{10,11},{12,13},{... | collective-permute-start | bytes 786440 | tf_op jit(solution)/shard_map/ppermute | solution.py:30
  5.8 1.3 collective-permute-start.4
  7.1 2.7 %constant_dynamic-slice_fusion = (bf16[128,2048]{1,0:T(8,128)(2,1)}, bf16[128,2048]{1,0:T(8,128)(2,1)}, bf16[128,2048]{1,0:T(8,128)(2,1)S(1)}, bf16[128,2048]{1,0:T(8,128)(2,1)}) fusion(bf16[128,8192]{1,0:T(8,128)(2,1)} %param.6, s32[]{:T(128)S(6)} %select_n.54, s32[]{:T(128)S(6)} %select_n.60, s32[]{:T(128)S(6)} %select_n.61, s32[]{:T(128)S(6)} %select_n.57), kind=kLoop, calls=%fused_computation.27 | loop fusion | bytes 4194320 | tf_op jit(solution)/shard_map/dynamic_slice | solution.py:109
  9.8 2.1 %collective-permute-start.10 = (bf16[128,2048]{1,0:T(8,128)(2,1)}, bf16[128,2048]{1,0:T(8,128)(2,1)S(1)}, u32[]{:S(2)}, u32[]{:S(2)}) collective-permute-start(bf16[128,2048]{1,0:T(8,128)(2,1)} %get-tuple-element.18), channel_id=1, source_target_pairs={{0,1},{1,2},{2,3},{3,0},{4,5},{5,6},{6,7},{7,4},{8,9},{9,10},{10,1... | collective-permute-start | bytes 1572872 | tf_op jit(solution)/shard_map/ppermute | solution.py:21
  11.9 2.3 %collective-permute-start.11 = (bf16[128,2048]{1,0:T(8,128)(2,1)}, bf16[128,2048]{1,0:T(8,128)(2,1)S(1)}, u32[]{:S(2)}, u32[]{:S(2)}) collective-permute-start(bf16[128,2048]{1,0:T(8,128)(2,1)} %get-tuple-element.20), channel_id=1, source_target_pairs={{0,2},{1,3},{2,0},{3,1},{4,6},{5,7},{6,4},{7,5},{8,10},{9,11},{10,... | collective-permute-start | bytes 1572872 | tf_op jit(solution)/shard_map/ppermute | solution.py:21
  15.8 1.4 %collective-permute-start.6 = (bf16[128,1024]{1,0:T(8,128)(2,1)}, bf16[128,1024]{1,0:T(8,128)(2,1)S(1)}, u32[]{:S(2)}, u32[]{:S(2)}) collective-permute-start(bf16[128,1024]{1,0:T(8,128)(2,1)} %collective-permute-done.4), channel_id=1, source_target_pairs={{1,0},{2,1},{5,4},{6,5},{9,8},{10,9},{13,12},{14,13},{17,16},{18,1... | collective-permute-start | bytes 786440 | tf_op jit(solution)/shard_map/ppermute | solution.py:30
  17.3 3.7 %convolution_convert_fusion.3 = bf16[128,2048]{1,0:T(8,128)(2,1)S(1)} fusion(bf16[128,1024]{1,0:T(8,128)(2,1)S(1)} %fusion.4.refs_4_, bf16[2048,1024]{1,0:T(8,128)(2,1)} %param.9), kind=kOutput, calls=%fused_computation.4 | convolution fusion | flops 537133056 | bytes 4980736 | tf_op jit(solution)/shard_map/dot_general | solution.py:112
  21.0 4.0 %collective-permute-start = (bf16[128,2048]{1,0:T(8,128)(2,1)S(1)}, bf16[128,2048]{1,0:T(8,128)(2,1)S(1)}, u32[]{:S(2)}, u32[]{:S(2)}) collective-permute-start(bf16[128,2048]{1,0:T(8,128)(2,1)S(1)} %convolution_convert_fusion.3), channel_id=1, source_target_pairs={{4,0},{5,1},{6,2},{7,3},{8,4},{9,5},{10,6},{11,7},{12,8},{13,9},{1... | collective-permute-start | bytes 1572872 | tf_op jit(solution)/shard_map/ppermute | solution.py:40
  25.0 30.3 %collective-permute-done.6 = bf16[128,1024]{1,0:T(8,128)(2,1)S(1)} collective-permute-done((bf16[128,1024]{1,0:T(8,128)(2,1)}, bf16[128,1024]{1,0:T(8,128)(2,1)S(1)}, u32[]{:S(2)}, u32[]{:S(2)}) %collective-permute-start.6) | collective-permute-done | bytes 262176 | tf_op jit(solution)/shard_map/ppermute | solution.py:30
  55.2 1.3 collective-permute-start.8
  56.6 2.3 %convolution_convert_fusion.1 = bf16[128,2048]{1,0:T(8,128)(2,1)} fusion(bf16[128,1024]{1,0:T(8,128)(2,1)S(1)} %broadcast_select_fusion.1.refs_6_, bf16[2048,1024]{1,0:T(8,128)(2,1)S(1)} %copy-done.1), kind=kOutput, calls=%fused_computation.2 | convolution fusion | flops 537133056 | bytes 4980736 | tf_op jit(solution)/shard_map/dot_general | solution.py:112
  59.9 13.8 %collective-permute-done.8 = bf16[128,1024]{1,0:T(8,128)(2,1)S(1)} collective-permute-done((bf16[128,1024]{1,0:T(8,128)(2,1)S(1)}, bf16[128,1024]{1,0:T(8,128)(2,1)S(1)}, u32[]{:S(2)}, u32[]{:S(2)}) %collective-permute-start.8) | collective-permute-done | bytes 262176 | tf_op jit(solution)/shard_map/ppermute | solution.py:30
  73.7 4.4 %collective-permute-start.7 = (bf16[128,2048]{1,0:T(8,128)(2,1)}, bf16[128,2048]{1,0:T(8,128)(2,1)}, u32[]{:S(2)}, u32[]{:S(2)}) collective-permute-start(bf16[128,2048]{1,0:T(8,128)(2,1)} %convolution_convert_fusion.1), channel_id=1, source_target_pairs={{4,2},{5,3},{6,0},{7,1},{8,6},{9,7},{10,4},{11,5},{12,10},{13,11},... | collective-permute-start | bytes 1572872 | tf_op jit(solution)/shard_map/ppermute | solution.py:40
  79.2 6.4 %gradient_and_sums.1 = (f32[2048,1024]{1,0:T(8,128)S(1)}, f32[2048,1]{1,0:T(8,128)S(1)}, f32[1,1024]{1,0:T(1,128)S(1)}, f32[1,1024]{1,0:T(1,128)S(1)}) custom-call(bf16[128,2048]{1,0:T(8,128)(2,1)S(1)} %get-tuple-element.19.refs_0_, bf16[128,2048]{1,0:T(8,128)(2,1)S(1)} %collective-permute-done.10.refs_1_, ...), custom_call_target="tpu_custom_call" | custom-call | flops 2147483648 | bytes 11534336 | tf_op jit(solution)/shard_map/gradient_and_sums/pallas_call | solution.py:74
  85.6 1.6 %fusion.9 = (f32[2048]{0:T(1024)}, f32[]{:T(128)}, f32[2048]{0:T(1024)S(1)}) fusion(f32[2048,1]{1,0:T(8,128)S(1)} %get-tuple-element.9), kind=kLoop, calls=%fused_computation.35 | loop fusion | flops 2047 | bytes 24580 | tf_op jit(solution)/shard_map/gradient_and_sums/pallas_call | solution.py:74
  88.0 8.2 %collective-permute-start.14 = (f32[24,128]{1,0:T(8,128)S(1)}, f32[24,128]{1,0:T(8,128)S(1)}, u32[]{:S(2)}, u32[]{:S(2)}) collective-permute-start(f32[24,128]{1,0:T(8,128)S(1)} %maximum_maximum_fusion), channel_id=1, source_target_pairs={{0,2},{1,3},{2,0},{3,1},{4,6},{5,7},{6,4},{7,5},{8,10},{9,11},{10,... | collective-permute-start | bytes 36872 | tf_op jit(solution)/shard_map/ppermute | solution.py:21
  97.3 1.5 %convolution_convert_fusion.2 = bf16[128,2048]{1,0:T(8,128)(2,1)S(1)} fusion(bf16[128,1024]{1,0:T(8,128)(2,1)S(1)} %broadcast_select_fusion.2.refs_7_, bf16[2048,1024]{1,0:T(8,128)(2,1)S(1)} %copy-done.1), kind=kOutput, calls=%fused_computation.3 | convolution fusion | flops 537133056 | bytes 4980736 | tf_op jit(solution)/shard_map/dot_general | solution.py:112
  98.8 1.5 %convolution_convert_fusion = bf16[128,2048]{1,0:T(8,128)(2,1)S(1)} fusion(bf16[128,1024]{1,0:T(8,128)(2,1)S(1)} %broadcast_select_fusion.refs_5_, bf16[2048,1024]{1,0:T(8,128)(2,1)S(1)} %copy-done.1), kind=kOutput, calls=%fused_computation.1 | convolution fusion | flops 537133056 | bytes 4980736 | tf_op jit(solution)/shard_map/dot_general | solution.py:112
  100.3 2.3 %collective-permute-start.5 = (bf16[128,2048]{1,0:T(8,128)(2,1)S(1)}, bf16[128,2048]{1,0:T(8,128)(2,1)S(1)}, u32[]{:S(2)}, u32[]{:S(2)}) collective-permute-start(bf16[128,2048]{1,0:T(8,128)(2,1)S(1)} %convolution_convert_fusion.2), channel_id=1, source_target_pairs={{4,1},{5,2},{6,3},{7,0},{8,5},{9,6},{10,7},{11,4},{12,9},{13,10},{... | collective-permute-start | bytes 1572872 | tf_op jit(solution)/shard_map/ppermute | solution.py:40
  103.3 1.9 %collective-permute-start.9 = (bf16[128,2048]{1,0:T(8,128)(2,1)S(1)}, bf16[128,2048]{1,0:T(8,128)(2,1)S(1)}, u32[]{:S(2)}, u32[]{:S(2)}) collective-permute-start(bf16[128,2048]{1,0:T(8,128)(2,1)S(1)} %convolution_convert_fusion), channel_id=1, source_target_pairs={{4,3},{5,0},{6,1},{7,2},{8,7},{9,4},{10,5},{11,6},{12,11},{13,8},{... | collective-permute-start | bytes 1572872 | tf_op jit(solution)/shard_map/ppermute | solution.py:40
  107.9 5.3 %multiply_convert_fusion = bf16[2048,1024]{1,0:T(8,128)(2,1)} fusion(f32[2048,1024]{1,0:T(8,128)} %copy-done, f32[1024]{0:T(1024)S(1)} %rsqrt_multiply_fusion, f32[2048]{0:T(1024)S(1)} %get-tuple-element.14), kind=kLoop, calls=%fused_computation | loop fusion | flops 6291456 | bytes 12595200 | tf_op jit(solution)/shard_map/convert_element_type | solution.py:148
  113.2 6.9 %collective-permute-done.5 = bf16[128,2048]{1,0:T(8,128)(2,1)S(1)} collective-permute-done((bf16[128,2048]{1,0:T(8,128)(2,1)S(1)}, bf16[128,2048]{1,0:T(8,128)(2,1)S(1)}, u32[]{:S(2)}, u32[]{:S(2)}) %collective-permute-start.5) | collective-permute-done | bytes 524320 | tf_op jit(solution)/shard_map/ppermute | solution.py:40
  121.3 8.6 %collective-permute-done.9 = bf16[128,2048]{1,0:T(8,128)(2,1)S(1)} collective-permute-done((bf16[128,2048]{1,0:T(8,128)(2,1)S(1)}, bf16[128,2048]{1,0:T(8,128)(2,1)S(1)}, u32[]{:S(2)}, u32[]{:S(2)}) %collective-permute-start.9) | collective-permute-done | bytes 524320 | tf_op jit(solution)/shard_map/ppermute | solution.py:40
  129.9 1.3 copy-done.4
  (53 shorter events, 9.7 us)
Async XLA Ops:
  0.6 13.9 %copy-start.6 = (f32[2048]{0:T(1024)S(1)}, f32[2048]{0:T(1024)}, u32[]{:S(2)}) copy-start(f32[2048]{0:T(1024)} %param.10) | copy-start | bytes 24580
  1.8 13.1 %collective-permute-start.1 = (bf16[128,1024]{1,0:T(8,128)(2,1)S(1)}, bf16[128,1024]{1,0:T(8,128)(2,1)}, u32[]{:S(2)}, u32[]{:S(2)}) collective-permute-start(bf16[128,1024]{1,0:T(8,128)(2,1)S(1)} %fusion.4.refs_4_), channel_id=1, source_target_pairs={{0,1},{1,2},{2,3},{4,5},{5,6},{6,7},{8,9},{9,10},{10,11},{12,13},{... | collective-permute-start | bytes 786440 | tf_op jit(solution)/shard_map/ppermute | solution.py:30
  5.8 10.0 %collective-permute-start.4 = (bf16[128,1024]{1,0:T(8,128)(2,1)S(1)}, bf16[128,1024]{1,0:T(8,128)(2,1)}, u32[]{:S(2)}, u32[]{:S(2)}) collective-permute-start(bf16[128,1024]{1,0:T(8,128)(2,1)S(1)} %fusion.4.refs_4_), channel_id=1, source_target_pairs={{1,0},{2,1},{3,2},{5,4},{6,5},{7,6},{9,8},{10,9},{11,10},{13,12},{... | collective-permute-start | bytes 786440 | tf_op jit(solution)/shard_map/ppermute | solution.py:30
  9.8 69.3 %collective-permute-start.10 = (bf16[128,2048]{1,0:T(8,128)(2,1)}, bf16[128,2048]{1,0:T(8,128)(2,1)S(1)}, u32[]{:S(2)}, u32[]{:S(2)}) collective-permute-start(bf16[128,2048]{1,0:T(8,128)(2,1)} %get-tuple-element.18), channel_id=1, source_target_pairs={{0,1},{1,2},{2,3},{3,0},{4,5},{5,6},{6,7},{7,4},{8,9},{9,10},{10,1... | collective-permute-start | bytes 1572872 | tf_op jit(solution)/shard_map/ppermute | solution.py:21
  11.9 67.2 %collective-permute-start.11 = (bf16[128,2048]{1,0:T(8,128)(2,1)}, bf16[128,2048]{1,0:T(8,128)(2,1)S(1)}, u32[]{:S(2)}, u32[]{:S(2)}) collective-permute-start(bf16[128,2048]{1,0:T(8,128)(2,1)} %get-tuple-element.20), channel_id=1, source_target_pairs={{0,2},{1,3},{2,0},{3,1},{4,6},{5,7},{6,4},{7,5},{8,10},{9,11},{10,... | collective-permute-start | bytes 1572872 | tf_op jit(solution)/shard_map/ppermute | solution.py:21
  14.2 65.0 %collective-permute-start.12 = (bf16[128,2048]{1,0:T(8,128)(2,1)}, bf16[128,2048]{1,0:T(8,128)(2,1)S(1)}, u32[]{:S(2)}, u32[]{:S(2)}) collective-permute-start(bf16[128,2048]{1,0:T(8,128)(2,1)} %get-tuple-element.17), channel_id=1, source_target_pairs={{0,3},{1,0},{2,1},{3,2},{4,7},{5,4},{6,5},{7,6},{8,11},{9,8},{10,9... | collective-permute-start | bytes 1572872 | tf_op jit(solution)/shard_map/ppermute | solution.py:21
  15.0 41.6 %copy-start.1 = (bf16[2048,1024]{1,0:T(8,128)(2,1)S(1)}, bf16[2048,1024]{1,0:T(8,128)(2,1)}, u32[]{:S(2)}) copy-start(bf16[2048,1024]{1,0:T(8,128)(2,1)} %param.9) | copy-start | bytes 12582916
  15.0 6.0 %collective-permute-start.2 = (bf16[128,1024]{1,0:T(8,128)(2,1)}, bf16[128,1024]{1,0:T(8,128)(2,1)S(1)}, u32[]{:S(2)}, u32[]{:S(2)}) collective-permute-start(bf16[128,1024]{1,0:T(8,128)(2,1)} %collective-permute-done.1), channel_id=1, source_target_pairs={{1,2},{2,3},{5,6},{6,7},{9,10},{10,11},{13,14},{14,15},{17,18},{18... | collective-permute-start | bytes 786440 | tf_op jit(solution)/shard_map/ppermute | solution.py:30
  15.8 39.4 %collective-permute-start.6 = (bf16[128,1024]{1,0:T(8,128)(2,1)}, bf16[128,1024]{1,0:T(8,128)(2,1)S(1)}, u32[]{:S(2)}, u32[]{:S(2)}) collective-permute-start(bf16[128,1024]{1,0:T(8,128)(2,1)} %collective-permute-done.4), channel_id=1, source_target_pairs={{1,0},{2,1},{5,4},{6,5},{9,8},{10,9},{13,12},{14,13},{17,16},{18,1... | collective-permute-start | bytes 786440 | tf_op jit(solution)/shard_map/ppermute | solution.py:30
  21.0 37.9 %collective-permute-start = (bf16[128,2048]{1,0:T(8,128)(2,1)S(1)}, bf16[128,2048]{1,0:T(8,128)(2,1)S(1)}, u32[]{:S(2)}, u32[]{:S(2)}) collective-permute-start(bf16[128,2048]{1,0:T(8,128)(2,1)S(1)} %convolution_convert_fusion.3), channel_id=1, source_target_pairs={{4,0},{5,1},{6,2},{7,3},{8,4},{9,5},{10,6},{11,7},{12,8},{13,9},{1... | collective-permute-start | bytes 1572872 | tf_op jit(solution)/shard_map/ppermute | solution.py:40
  55.2 18.5 %collective-permute-start.8 = (bf16[128,1024]{1,0:T(8,128)(2,1)S(1)}, bf16[128,1024]{1,0:T(8,128)(2,1)S(1)}, u32[]{:S(2)}, u32[]{:S(2)}) collective-permute-start(bf16[128,1024]{1,0:T(8,128)(2,1)S(1)} %collective-permute-done.6), channel_id=1, source_target_pairs={{1,0},{5,4},{9,8},{13,12},{17,16},{21,20},{25,24},{29,28}} | collective-permute-start | bytes 786440 | tf_op jit(solution)/shard_map/ppermute | solution.py:30
  58.9 19.2 %collective-permute-start.3 = (bf16[128,1024]{1,0:T(8,128)(2,1)S(1)}, bf16[128,1024]{1,0:T(8,128)(2,1)S(1)}, u32[]{:S(2)}, u32[]{:S(2)}) collective-permute-start(bf16[128,1024]{1,0:T(8,128)(2,1)S(1)} %collective-permute-done.2), channel_id=1, source_target_pairs={{2,3},{6,7},{10,11},{14,15},{18,19},{22,23},{26,27},{30,31}} | collective-permute-start | bytes 786440 | tf_op jit(solution)/shard_map/ppermute | solution.py:30
  59.8 43.4 %copy-start.2 = (bf16[128,8192]{1,0:T(8,128)(2,1)}, bf16[128,8192]{1,0:T(8,128)(2,1)S(1)}, u32[]{:S(2)}) copy-start(bf16[128,8192]{1,0:T(8,128)(2,1)S(1)} %constant_dynamic-update-slice_fusion.3) | copy-start | bytes 6291460
  73.7 46.5 %collective-permute-start.7 = (bf16[128,2048]{1,0:T(8,128)(2,1)}, bf16[128,2048]{1,0:T(8,128)(2,1)}, u32[]{:S(2)}, u32[]{:S(2)}) collective-permute-start(bf16[128,2048]{1,0:T(8,128)(2,1)} %convolution_convert_fusion.1), channel_id=1, source_target_pairs={{4,2},{5,3},{6,0},{7,1},{8,6},{9,7},{10,4},{11,5},{12,10},{13,11},... | collective-permute-start | bytes 1572872 | tf_op jit(solution)/shard_map/ppermute | solution.py:40
  85.6 14.7 %copy-start = (f32[2048,1024]{1,0:T(8,128)}, f32[2048,1024]{1,0:T(8,128)S(1)}, u32[]{:S(2)}) copy-start(f32[2048,1024]{1,0:T(8,128)S(1)} %get-tuple-element.8) | copy-start | bytes 25165828
  88.0 17.8 %copy-start.7 = (f32[1024]{0:T(1024)S(1)}, f32[1024]{0:T(1024)}, u32[]{:S(2)}) copy-start(f32[1024]{0:T(1024)} %param.11) | copy-start | bytes 12292
  88.0 15.2 %collective-permute-start.13 = (f32[24,128]{1,0:T(8,128)S(1)}, f32[24,128]{1,0:T(8,128)S(1)}, u32[]{:S(2)}, u32[]{:S(2)}) collective-permute-start(f32[24,128]{1,0:T(8,128)S(1)} %maximum_maximum_fusion), channel_id=1, source_target_pairs={{0,1},{1,2},{2,3},{3,0},{4,5},{5,6},{6,7},{7,4},{8,9},{9,10},{10,1... | collective-permute-start | bytes 36872 | tf_op jit(solution)/shard_map/ppermute | solution.py:21
  88.0 17.2 %collective-permute-start.14 = (f32[24,128]{1,0:T(8,128)S(1)}, f32[24,128]{1,0:T(8,128)S(1)}, u32[]{:S(2)}, u32[]{:S(2)}) collective-permute-start(f32[24,128]{1,0:T(8,128)S(1)} %maximum_maximum_fusion), channel_id=1, source_target_pairs={{0,2},{1,3},{2,0},{3,1},{4,6},{5,7},{6,4},{7,5},{8,10},{9,11},{10,... | collective-permute-start | bytes 36872 | tf_op jit(solution)/shard_map/ppermute | solution.py:21
  96.2 9.0 %collective-permute-start.15 = (f32[24,128]{1,0:T(8,128)S(1)}, f32[24,128]{1,0:T(8,128)S(1)}, u32[]{:S(2)}, u32[]{:S(2)}) collective-permute-start(f32[24,128]{1,0:T(8,128)S(1)} %maximum_maximum_fusion), channel_id=1, source_target_pairs={{0,3},{1,0},{2,1},{3,2},{4,7},{5,4},{6,5},{7,6},{8,11},{9,8},{10,9... | collective-permute-start | bytes 36872 | tf_op jit(solution)/shard_map/ppermute | solution.py:21
  100.3 19.8 %collective-permute-start.5 = (bf16[128,2048]{1,0:T(8,128)(2,1)S(1)}, bf16[128,2048]{1,0:T(8,128)(2,1)S(1)}, u32[]{:S(2)}, u32[]{:S(2)}) collective-permute-start(bf16[128,2048]{1,0:T(8,128)(2,1)S(1)} %convolution_convert_fusion.2), channel_id=1, source_target_pairs={{4,1},{5,2},{6,3},{7,0},{8,5},{9,6},{10,7},{11,4},{12,9},{13,10},{... | collective-permute-start | bytes 1572872 | tf_op jit(solution)/shard_map/ppermute | solution.py:40
  103.3 26.6 %collective-permute-start.9 = (bf16[128,2048]{1,0:T(8,128)(2,1)S(1)}, bf16[128,2048]{1,0:T(8,128)(2,1)S(1)}, u32[]{:S(2)}, u32[]{:S(2)}) collective-permute-start(bf16[128,2048]{1,0:T(8,128)(2,1)S(1)} %convolution_convert_fusion), channel_id=1, source_target_pairs={{4,3},{5,0},{6,1},{7,2},{8,7},{9,4},{10,5},{11,6},{12,11},{13,8},{... | collective-permute-start | bytes 1572872 | tf_op jit(solution)/shard_map/ppermute | solution.py:40
  106.5 6.8 %copy-start.5 = (f32[1024]{0:T(1024)}, f32[1024]{0:T(1024)S(1)}, u32[]{:S(2)}) copy-start(f32[1024]{0:T(1024)S(1)} %get-tuple-element.16) | copy-start | bytes 12292
  107.9 12.2 %copy-start.3 = (bf16[128,8192]{1,0:T(8,128)(2,1)S(1)}, bf16[128,8192]{1,0:T(8,128)(2,1)}, u32[]{:S(2)}) copy-start(bf16[128,8192]{1,0:T(8,128)(2,1)} %copy-done.2) | copy-start | bytes 6291460
  129.9 1.3 %copy-start.4 = (bf16[128,8192]{1,0:T(8,128)(2,1)}, bf16[128,8192]{1,0:T(8,128)(2,1)S(1)}, u32[]{:S(2)}) copy-start(bf16[128,8192]{1,0:T(8,128)(2,1)S(1)} %constant_dynamic-update-slice_fusion) | copy-start | bytes 6291460

commit v2 on v1

v2 whole, which is shorter than its diff:
```python
import functools

import jax
import jax.numpy as jnp
from jax import lax
from jax.experimental import pallas as pl
from jax.experimental.pallas import tpu as pltpu
from jax.sharding import PartitionSpec as P

BETA_TWO = 0.75
TINY_ADD = 1e-30
SECTION, DP = "section", "dp"
MIB = 1024 * 1024
NO_COST = pl.CostEstimate(flops=0, bytes_accessed=0, transcendentals=0)


def after(value, *others):
    return lax.optimization_barrier((value, *others))[0]


def ring(value, steps):
    count = lax.axis_size(DP)
    return lax.ppermute(value, DP, [(i, (i + steps) % count) for i in range(count)])


def reach(value, steps):
    count = lax.axis_size(DP)
    return lax.ppermute(
        value, DP, [(i, i + steps) for i in range(count) if 0 <= i + steps < count]
    )


def hop(value, origin, steps):
    count = lax.axis_size(DP)
    if steps > 0:
        pairs = [(i, i + 1) for i in range(origin, count - 1)]
    else:
        pairs = [(i, i - 1) for i in range(1, count - origin)]
    return lax.ppermute(value, DP, pairs)


def everyone(value):
    count = lax.axis_size(DP)
    if count & (count - 1):
        return lax.psum(value, DP)
    reach_of = 1
    while reach_of < count:
        value = value + lax.ppermute(value, DP, [(i, i ^ reach_of) for i in range(count)])
        reach_of *= 2
    return value


def hand_over(value, steps):
    count, sections = lax.axis_size(DP), lax.axis_size(SECTION)
    pairs = [
        (s * count + i, (s - 1) * count + (i + steps) % count)
        for s in range(1, sections)
        for i in range(count)
    ]
    return lax.ppermute(value, (SECTION, DP), pairs)


def gradient_kernel(parts, sub, *refs):
    xs, cs = refs[:parts], refs[parts : 2 * parts]
    state_ref, scaled_ref, row_ref, sums_ref = refs[2 * parts :]
    block, units = scaled_ref.shape
    c = jnp.concatenate([r[...] for r in cs], axis=0)
    totals = [jnp.zeros((1, units), jnp.float32)] * 2 + [jnp.zeros((1, 1), jnp.float32)]
    for at in range(0, block, sub):
        here = slice(at, at + sub)
        x = jnp.concatenate([r[:, here] for r in xs], axis=0)
        grad = lax.dot_general(
            x, c, (((0,), (0,)), ((), ())), preferred_element_type=jnp.float32
        )
        squares = grad * grad + TINY_ADD
        row = BETA_TWO * state_ref[here, :] + (1.0 - BETA_TWO) * (
            jnp.sum(squares, axis=1, keepdims=True) / float(units)
        )
        scaled = grad * lax.rsqrt(row)
        scaled_ref[here, :] = scaled.astype(scaled_ref.dtype)
        row_ref[:, here] = jnp.broadcast_to(row, (sub, 128)).T[:1, :]
        totals[0] += jnp.sum(squares, axis=0, keepdims=True)
        totals[1] += jnp.sum(scaled * scaled, axis=0, keepdims=True)
        totals[2] += jnp.sum(row, axis=0, keepdims=True)

    @pl.when(pl.program_id(0) == 0)
    def _():
        sums_ref[...] = jnp.zeros_like(sums_ref)

    sums_ref[0:1, :] += totals[0]
    sums_ref[1:2, :] += totals[1]
    sums_ref[2:3, :] += jnp.broadcast_to(totals[2], (1, units))


def gradient_call(xs, cs, row_state, block=1024):
    parts = len(xs)
    tokens, rows = xs[0].shape
    units = cs[0].shape[1]
    block = min(block, rows)
    return pl.pallas_call(
        functools.partial(gradient_kernel, parts, min(256, block)),
        grid=(rows // block,),
        in_specs=[pl.BlockSpec((tokens, block), lambda i: (0, i))] * parts
        + [pl.BlockSpec((tokens, units), lambda i: (0, 0))] * parts
        + [pl.BlockSpec((block, 1), lambda i: (i, 0))],
        out_specs=[
            pl.BlockSpec((block, units), lambda i: (i, 0)),
            pl.BlockSpec((1, block), lambda i: (0, i)),
            pl.BlockSpec((8, units), lambda i: (0, 0)),
        ],
        out_shape=[
            jax.ShapeDtypeStruct((rows, units), jnp.bfloat16),
            jax.ShapeDtypeStruct((1, rows), jnp.float32),
            jax.ShapeDtypeStruct((8, units), jnp.float32),
        ],
        compiler_params=pltpu.CompilerParams(vmem_limit_bytes=24 * MIB),
        cost_estimate=NO_COST,
        name="gradient_and_sums",
    )(*xs, *cs, row_state[:, None])


def step_kernel(width, sums_ref, state_ref, scaled_ref, step_ref, col_ref, factor_ref):
    units = scaled_ref.shape[1]

    @pl.when(pl.program_id(0) == 0)
    def _():
        col = BETA_TWO * state_ref[...] + (1.0 - BETA_TWO) * (sums_ref[0:1, :] / width)
        col_ref[...] = col
        average = sums_ref[2:3, :] / width
        grand = jnp.sum(average * sums_ref[1:2, :] / col, axis=1, keepdims=True)
        root_mean = jnp.sqrt(grand / (width * float(units)))
        factor_ref[...] = lax.rsqrt(col) * jnp.sqrt(average) / jnp.maximum(1.0, root_mean)

    step_ref[...] = (scaled_ref[...] * factor_ref[...]).astype(step_ref.dtype)


def step_call(scaled, sums, col_state, width, block=512):
    rows, units = scaled.shape
    block = min(block, rows)
    return pl.pallas_call(
        functools.partial(step_kernel, float(width)),
        grid=(rows // block,),
        in_specs=[
            pl.BlockSpec((8, units), lambda i: (0, 0)),
            pl.BlockSpec((1, units), lambda i: (0, 0)),
            pl.BlockSpec((block, units), lambda i: (i, 0)),
        ],
        out_specs=[
            pl.BlockSpec((block, units), lambda i: (i, 0)),
            pl.BlockSpec((1, units), lambda i: (0, 0)),
        ],
        out_shape=[
            jax.ShapeDtypeStruct((rows, units), jnp.bfloat16),
            jax.ShapeDtypeStruct((1, units), jnp.float32),
        ],
        scratch_shapes=[pltpu.VMEM((1, units), jnp.float32)],
        compiler_params=pltpu.CompilerParams(vmem_limit_bytes=16 * MIB),
        cost_estimate=NO_COST,
        name="scaled_step",
    )(sums, col_state[None, :], scaled)


def lowered_kernel(cot_ref, weight_ref, out_ref):
    out_ref[...] = lax.dot_general(
        cot_ref[...], weight_ref[...], (((1,), (1,)), ((), ())), preferred_element_type=jnp.float32
    ).astype(out_ref.dtype)


def lowered(cot, weight, block=512):
    tokens, units = cot.shape
    rows = weight.shape[0]
    block = min(block, rows)
    return pl.pallas_call(
        lowered_kernel,
        grid=(rows // block,),
        in_specs=[
            pl.BlockSpec((tokens, units), lambda i: (0, 0)),
            pl.BlockSpec((block, units), lambda i: (i, 0)),
        ],
        out_specs=pl.BlockSpec((tokens, block), lambda i: (0, i)),
        out_shape=jax.ShapeDtypeStruct((tokens, rows), jnp.bfloat16),
        compiler_params=pltpu.CompilerParams(vmem_limit_bytes=16 * MIB),
        cost_estimate=NO_COST,
        name="lowered_block",
    )(cot, weight)


def assemble_kernel(count, me_ref, *refs):
    parts, out_ref = refs[:count], refs[count]
    steps = lax.rem(me_ref[0] - pl.program_id(0) + count, count)
    for k in range(count):
        @pl.when(steps == k)
        def _(k=k):
            out_ref[...] = parts[k][...]


def assemble(parts, me):
    count = len(parts)
    tokens, rows = parts[0].shape
    return pl.pallas_call(
        functools.partial(assemble_kernel, count),
        grid=(count,),
        in_specs=[pl.BlockSpec(memory_space=pltpu.SMEM)]
        + [pl.BlockSpec((tokens, rows), lambda i: (0, 0))] * count,
        out_specs=pl.BlockSpec((tokens, rows), lambda i: (0, i)),
        out_shape=jax.ShapeDtypeStruct((tokens, count * rows), parts[0].dtype),
        compiler_params=pltpu.CompilerParams(vmem_limit_bytes=16 * MIB),
        cost_estimate=NO_COST,
        name="assemble",
    )(me[None], *parts)


def local(inputs, hidden_grad, gate_pre, up_weight, row_state, col_state):
    count = lax.axis_size(DP)
    me = lax.axis_index(DP)
    tokens, width = inputs.shape
    rows, units = up_weight.shape

    def columns_of(owner):
        return lax.dynamic_slice_in_dim(inputs, owner * rows, rows, axis=1)

    cotangent = (
        hidden_grad.astype(jnp.float32) * jax.nn.silu(gate_pre.astype(jnp.float32))
    ).astype(jnp.bfloat16)

    ahead = {1: reach(cotangent, 1), 2: reach(cotangent, 2)}
    behind = {1: reach(cotangent, -1), 2: reach(cotangent, -2)}
    for j in range(3, count):
        ahead[j] = hop(ahead[j - 1], j - 1, 1)
        behind[j] = hop(behind[j - 1], j - 1, -1)
    cots = [cotangent] + [
        jnp.where(me >= k, ahead[k], behind[count - k]) for k in range(1, count)
    ]
    order = list(range(1, count, 2)) + list(range(2, count, 2))
    xs = {}
    for k in order:
        xs[k] = ring(after(columns_of(lax.rem(me + k, count)), cotangent), k)
    xs[0] = after(columns_of(me), ahead[1])
    xs = [xs[k] for k in range(count)]

    low = [lowered(cots[(count - k) % count], up_weight) for k in range(count)]
    sent = [hand_over(low[k], k) for k in range(count)]

    def update(xs, cots, row_state):
        scaled, row_new, sums = gradient_call(xs, cots, row_state)
        return scaled, row_new, everyone(sums)

    def nothing(xs, cots, row_state):
        return (
            jnp.zeros((rows, units), jnp.bfloat16),
            jnp.zeros((1, rows), jnp.float32),
            jnp.zeros((8, units), jnp.float32),
        )

    scaled, row_new, total = lax.cond(
        lax.optimization_barrier(me) < count, update, nothing, xs, cots, row_state
    )
    upstream = assemble([sent[k] for k in range(count)], me)
    step_out, col_new = step_call(scaled, after(total, upstream), col_state, width)
    return (upstream, step_out, row_new.reshape(-1), col_new.reshape(-1))


def solution(mesh):
    blocks = P((SECTION, DP), None)
    vector = P((SECTION, DP))
    return jax.shard_map(
        local,
        mesh=mesh,
        in_specs=(blocks, blocks, blocks, blocks, vector, P(SECTION)),
        out_specs=(blocks, blocks, vector, P(SECTION)),
        check_vma=False,
    )
```

time: 132 us -> 127 us (0.962); the launches traced: 131 us -> 124 us
  waiting for transfers between devices: 59.6 us -> 24 us
  starting transfers between devices: 35.9 us -> 68.5 us
  Pallas kernels: 6.4 us -> 21.3 us
  matrix products: 9.04 us -> 0 us
  other arithmetic: 9.96 us -> 3.21 us
  between operations: 2.46 us -> 0.91 us
  local copies, waits for them, and re-layouts: 7.84 us -> 6.46 us
    ppermute x6 -> x2, waiting for transfers between devices: 44.1 us -> 7.86 us  [hop(): return lax.ppermute(value, DP, pairs)]
    ppermute x4, starting transfers between devices: 12.6 us -> 44.4 us  [hand_over(): return lax.ppermute(value, (SECTION, DP), pairs)]
    ppermute x0 -> x6, starting transfers between devices: none -> 19.3 us  [the longest x4 10.7 us: reach(): lax.ppermute(value, DP, [(i, i + steps) for i in range(count) if 0 <= i +...]
    ppermute x4, waiting for transfers between devices: 15.5 us -> 0.01 us  [hand_over(): return lax.ppermute(value, (SECTION, DP), pairs)]
    pallas_call x1 -> x7, Pallas kernels: 6.4 us -> 21.3 us  [the longest x4 9.66 us: lowered(): pl.pallas_call(lowered_kernel, grid=(rows // block,), in_specs=[pl.BlockS...]
    ppermute x6 -> x3, starting transfers between devices: 14 us -> 2.85 us  [ring(): lax.ppermute(value, DP, [(i, (i + steps) % count) for i in range(count)])]
    ppermute x0 -> x6, waiting for transfers between devices: none -> 9.54 us  [the longest x4 4.87 us: reach(): lax.ppermute(value, DP, [(i, i + steps) for i in range(count) if 0 <= i +...]
    dot_general x4 -> x0, matrix products: 9.04 us -> none  [lowered(): lax.dot_general(cot, up_weight, (((1,), (1,)), ((), ())), preferred_eleme...]
  transfers between devices with their start and end apart: 16 -> 15, of which waited for: 4 -> 5; matrix products, arithmetic and copies ran while one was open for 18% -> 4% of each run, Pallas kernels for 5% -> 12%
where the time goes in v2:
time: 127 us; the launch traced here: 124 us
  starting transfers between devices  68.5 us (54%)
  waiting for transfers between devices  24 us (19%)
  Pallas kernels  21.3 us (17%)
  local copies, waits for them, and re-layouts  6.46 us (5%)
  other arithmetic  3.21 us (3%)
    ppermute x4, starting transfers between devices, hand_over(): return lax.ppermute(value, (SECTION, DP), pairs)  44.4 us
    ppermute x4, starting transfers between devices, reach(): lax.ppermute(value, DP, [(i, i + steps) for i in range(count) if 0 <= i +...  10.7 us
    pallas_call x4, Pallas kernels, lowered(): pl.pallas_call(lowered_kernel, grid=(rows // block,), in_specs=[pl.BlockS...  9.66 us
    ppermute x2, starting transfers between devices, everyone(): lax.ppermute(value, DP, [(i, i ^ reach_of) for i in range(count)])  8.62 us
    ppermute x2, waiting for transfers between devices, hop(): return lax.ppermute(value, DP, pairs)  7.86 us
    ppermute x3, waiting for transfers between devices, ring(): lax.ppermute(value, DP, [(i, (i + steps) % count) for i in range(count)])  6.59 us
    pallas_call x1, Pallas kernels, gradient_call(): pl.pallas_call(functools.partial(gradient_kernel, parts, min(256, block))...  5.82 us
    ppermute x4, waiting for transfers between devices, reach(): lax.ppermute(value, DP, [(i, i + steps) for i in range(count) if 0 <= i +...  4.87 us
  transfers between devices with their start and end apart: 15, of which 5 were waited for; matrix products, arithmetic and copies ran while one was open for 4% of the time, Pallas kernels for 12%

profile of v2, /device:TPU:3, one launch (start us, length us, event | category | flops | bytes accessed | tf_op | source)
XLA Modules:
  0.0 124.5 jit_solution(17198412433200870375)
XLA Ops:
  1.8 1.3 %collective-permute-start.7 = (bf16[128,1024]{1,0:T(8,128)(2,1)S(1)}, bf16[128,1024]{1,0:T(8,128)(2,1)S(1)}, u32[]{:S(2)}, u32[]{:S(2)}) collective-permute-start(bf16[128,1024]{1,0:T(8,128)(2,1)S(1)} %fusion.4.cot_ref), channel_id=1, source_target_pairs={{2,0},{3,1},{6,4},{7,5},{10,8},{11,9},{14,12},{15,13},{18,16},{19,... | collective-permute-start | bytes 786440 | tf_op jit(solution)/shard_map/ppermute | solution.py:28
  3.1 3.2 %collective-permute-start.9 = (bf16[128,1024]{1,0:T(8,128)(2,1)S(1)}, bf16[128,1024]{1,0:T(8,128)(2,1)S(1)}, u32[]{:S(2)}, u32[]{:S(2)}) collective-permute-start(bf16[128,1024]{1,0:T(8,128)(2,1)S(1)} %fusion.4.cot_ref), channel_id=1, source_target_pairs={{0,1},{1,2},{2,3},{4,5},{5,6},{6,7},{8,9},{9,10},{10,11},{12,13},{... | collective-permute-start | bytes 786440 | tf_op jit(solution)/shard_map/ppermute | solution.py:28
  6.4 4.9 %collective-permute-start.3 = (bf16[128,1024]{1,0:T(8,128)(2,1)S(1)}, bf16[128,1024]{1,0:T(8,128)(2,1)S(1)}, u32[]{:S(2)}, u32[]{:S(2)}) collective-permute-start(bf16[128,1024]{1,0:T(8,128)(2,1)S(1)} %fusion.4.cot_ref), channel_id=1, source_target_pairs={{0,2},{1,3},{4,6},{5,7},{8,10},{9,11},{12,14},{13,15},{16,18},{17,... | collective-permute-start | bytes 786440 | tf_op jit(solution)/shard_map/ppermute | solution.py:28
  12.6 4.9 %collective-permute-done.7 = bf16[128,1024]{1,0:T(8,128)(2,1)S(1)} collective-permute-done((bf16[128,1024]{1,0:T(8,128)(2,1)S(1)}, bf16[128,1024]{1,0:T(8,128)(2,1)S(1)}, u32[]{:S(2)}, u32[]{:S(2)}) %collective-permute-start.7) | collective-permute-done | bytes 262176 | tf_op jit(solution)/shard_map/ppermute | solution.py:28
  18.7 2.9 %constant_dynamic-slice_fusion = (bf16[128,2048]{1,0:T(8,128)(2,1)}, bf16[128,2048]{1,0:T(8,128)(2,1)}, bf16[128,2048]{1,0:T(8,128)(2,1)}, bf16[128,2048]{1,0:T(8,128)(2,1)}) fusion(bf16[128,8192]{1,0:T(8,128)(2,1)} %param.8, s32[]{:T(128)S(6)} %select_n.41, s32[]{:T(128)S(6)} %select_n.39, s32[]{:T(128)S(6)} %select_n.38, s32[]{:T(128)S(6)} %select_n.40), kind=kLoop, calls=%fused_computation.10 | loop fusion | bytes 4194320 | tf_op jit(solution)/shard_map/dynamic_slice | solution.py:220
  21.6 2.8 %collective-permute-start.12 = (bf16[128,2048]{1,0:T(8,128)(2,1)}, bf16[128,2048]{1,0:T(8,128)(2,1)S(1)}, u32[]{:S(2)}, u32[]{:S(2)}) collective-permute-start(bf16[128,2048]{1,0:T(8,128)(2,1)} %get-tuple-element.46), channel_id=1, source_target_pairs={{0,1},{1,2},{2,3},{3,0},{4,5},{5,6},{6,7},{7,4},{8,9},{9,10},{10,1... | collective-permute-start | bytes 1572872 | tf_op jit(solution)/shard_map/ppermute | solution.py:23
  24.4 2.2 %copy-done = bf16[2048,1024]{1,0:T(8,128)(2,1)S(1)} copy-done((bf16[2048,1024]{1,0:T(8,128)(2,1)S(1)}, bf16[2048,1024]{1,0:T(8,128)(2,1)}, u32[]{:S(2)}) %copy-start) | copy-done | bytes 4194328
  26.6 2.0 %lowered_block.4 = bf16[128,2048]{1,0:T(8,128)(2,1)S(1)} custom-call(bf16[128,1024]{1,0:T(8,128)(2,1)S(1)} %fusion.4.cot_ref, bf16[2048,1024]{1,0:T(8,128)(2,1)S(1)} %copy-done), custom_call_target="tpu_custom_call" | custom-call | tf_op jit(solution)/shard_map/lowered_block/pallas_call | solution.py:173
  29.5 2.0 %lowered_block.6 = bf16[128,2048]{1,0:T(8,128)(2,1)S(1)} custom-call(bf16[128,1024]{1,0:T(8,128)(2,1)S(1)} %broadcast_select_fusion.1.cot_ref, bf16[2048,1024]{1,0:T(8,128)(2,1)S(1)} %copy-done), custom_call_target="tpu_custom_call" | custom-call | tf_op jit(solution)/shard_map/lowered_block/pallas_call | solution.py:173
  31.5 7.9 %collective-permute-done.10 = bf16[128,1024]{1,0:T(8,128)(2,1)} collective-permute-done((bf16[128,1024]{1,0:T(8,128)(2,1)S(1)}, bf16[128,1024]{1,0:T(8,128)(2,1)}, u32[]{:S(2)}, u32[]{:S(2)}) %collective-permute-start.10) | collective-permute-done | bytes 262176 | tf_op jit(solution)/shard_map/ppermute | solution.py:39
  40.4 4.2 %collective-permute-start.2 = (bf16[128,2048]{1,0:T(8,128)(2,1)S(1)}, bf16[128,2048]{1,0:T(8,128)(2,1)S(1)}, u32[]{:S(2)}, u32[]{:S(2)}) collective-permute-start(bf16[128,2048]{1,0:T(8,128)(2,1)S(1)} %lowered_block.4), channel_id=1, source_target_pairs={{4,0},{5,1},{6,2},{7,3},{8,4},{9,5},{10,6},{11,7},{12,8},{13,9},{1... | collective-permute-start | bytes 1572872 | tf_op jit(solution)/shard_map/ppermute | solution.py:60
  44.6 2.3 %collective-permute-start.8 = (bf16[128,2048]{1,0:T(8,128)(2,1)S(1)}, bf16[128,2048]{1,0:T(8,128)(2,1)S(1)}, u32[]{:S(2)}, u32[]{:S(2)}) collective-permute-start(bf16[128,2048]{1,0:T(8,128)(2,1)S(1)} %lowered_block.6), channel_id=1, source_target_pairs={{4,2},{5,3},{6,0},{7,1},{8,6},{9,7},{10,4},{11,5},{12,10},{13,11},... | collective-permute-start | bytes 1572872 | tf_op jit(solution)/shard_map/ppermute | solution.py:60
  47.9 2.8 %lowered_block.7 = bf16[128,2048]{1,0:T(8,128)(2,1)} custom-call(bf16[128,1024]{1,0:T(8,128)(2,1)S(1)} %broadcast_select_fusion.cot_ref, bf16[2048,1024]{1,0:T(8,128)(2,1)S(1)} %copy-done), custom_call_target="tpu_custom_call" | custom-call | tf_op jit(solution)/shard_map/lowered_block/pallas_call | solution.py:173
  50.7 2.8 %lowered_block.5 = bf16[128,2048]{1,0:T(8,128)(2,1)} custom-call(bf16[128,1024]{1,0:T(8,128)(2,1)S(1)} %broadcast_select_fusion.2.cot_ref, bf16[2048,1024]{1,0:T(8,128)(2,1)S(1)} %copy-done), custom_call_target="tpu_custom_call" | custom-call | tf_op jit(solution)/shard_map/lowered_block/pallas_call | solution.py:173
  53.5 3.0 %collective-permute-start.11 = (bf16[128,2048]{1,0:T(8,128)(2,1)}, bf16[128,2048]{1,0:T(8,128)(2,1)}, u32[]{:S(2)}, u32[]{:S(2)}) collective-permute-start(bf16[128,2048]{1,0:T(8,128)(2,1)} %lowered_block.7), channel_id=1, source_target_pairs={{4,3},{5,0},{6,1},{7,2},{8,7},{9,4},{10,5},{11,6},{12,11},{13,8},{... | collective-permute-start | bytes 1572872 | tf_op jit(solution)/shard_map/ppermute | solution.py:60
  56.6 6.6 %collective-permute-done.13 = bf16[128,2048]{1,0:T(8,128)(2,1)S(1)} collective-permute-done((bf16[128,2048]{1,0:T(8,128)(2,1)}, bf16[128,2048]{1,0:T(8,128)(2,1)S(1)}, u32[]{:S(2)}, u32[]{:S(2)}) %collective-permute-start.13) | collective-permute-done | bytes 524320 | tf_op jit(solution)/shard_map/ppermute | solution.py:23
  63.1 34.9 %collective-permute-start.6 = (bf16[128,2048]{1,0:T(8,128)(2,1)}, bf16[128,2048]{1,0:T(8,128)(2,1)}, u32[]{:S(2)}, u32[]{:S(2)}) collective-permute-start(bf16[128,2048]{1,0:T(8,128)(2,1)} %lowered_block.5), channel_id=1, source_target_pairs={{4,1},{5,2},{6,3},{7,0},{8,5},{9,6},{10,7},{11,4},{12,9},{13,10},{... | collective-permute-start | bytes 1572872 | tf_op jit(solution)/shard_map/ppermute | solution.py:60
  98.1 20.5 %conditional.1 = (bf16[2048,1024]{1,0:T(8,128)(2,1)S(1)}, f32[8,1024]{1,0:T(8,128)S(1)}, f32[2048]{0:T(1024)}) conditional(s32[]{:T(128)} %convert_element_type.15, () %tuple.23, (f32[2048]{0:T(1024)S(1)}, bf16[128,2048]{1,0:T(8,128)(2,1)}, bf16[128,2048]{1,0:T(8,128)(2,1)S(1)}, bf16[128,2048]{1,0:T(8,128)(2,1)S(1)}, bf16[128,2048]{1,0:T(8,128)(2,1)}, ...), branch_computations={%region_0.1_spmd, %region_1.2_spmd} | conditional | flops 16384 | bytes 4669600 | solution.py:255
  99.5 5.8 %gradient_and_sums.1 = (bf16[2048,1024]{1,0:T(8,128)(2,1)S(1)}, f32[1,2048]{1,0:T(1,128)}, f32[8,1024]{1,0:T(8,128)S(1)}) custom-call(bf16[128,2048]{1,0:T(8,128)(2,1)} %get-tuple-element.19.refs_0_, bf16[128,2048]{1,0:T(8,128)(2,1)} %copy-done.5, bf16[128,2048]{1,0:T(8,128)(2,1)} %copy-done.6, bf16[128,2048]{1,0:T(8,128)(2,1)} %get-tuple-element.22.refs_3_, ...), custom_call_target="tpu_custom_call" | custom-call | tf_op jit(solution)/shard_map/cond/branch_1_fun/gradient_and_sums/pallas_call | solution.py:100
  105.3 3.4 %collective-permute-done = f32[8,1024]{1,0:T(8,128)S(1)} collective-permute-done((f32[8,1024]{1,0:T(8,128)S(1)}, f32[8,1024]{1,0:T(8,128)S(1)}, u32[]{:S(2)}, u32[]{:S(2)}) %collective-permute-start) | collective-permute-done | bytes 32800 | tf_op jit(solution)/shard_map/cond/branch_1_fun/ppermute | solution.py:48
  108.7 8.6 %collective-permute-start.1 = (f32[8,1024]{1,0:T(8,128)S(1)}, f32[8,1024]{1,0:T(8,128)S(1)}, u32[]{:S(2)}, u32[]{:S(2)}) collective-permute-start(f32[8,1024]{1,0:T(8,128)S(1)} %add.21), channel_id=1, source_target_pairs={{0,2},{1,3},{2,0},{3,1},{4,6},{5,7},{6,4},{7,5},{8,10},{9,11},{10,... | collective-permute-start | bytes 98312 | tf_op jit(solution)/shard_map/cond/branch_1_fun/ppermute | solution.py:48
  117.3 1.3 %collective-permute-done.1 = f32[8,1024]{1,0:T(8,128)S(1)} collective-permute-done((f32[8,1024]{1,0:T(8,128)S(1)}, f32[8,1024]{1,0:T(8,128)S(1)}, u32[]{:S(2)}, u32[]{:S(2)}) %collective-permute-start.1) | collective-permute-done | bytes 32800 | tf_op jit(solution)/shard_map/cond/branch_1_fun/ppermute | solution.py:48
  118.6 3.1 %assemble.1 = bf16[128,8192]{1,0:T(8,128)(2,1)} custom-call(s32[1]{0:T(128)} %bitcast.2.me_ref, bf16[128,2048]{1,0:T(8,128)(2,1)S(1)} %collective-permute-done.2.refs_0_, bf16[128,2048]{1,0:T(8,128)(2,1)} %collective-permute-done.6.refs_1_, bf16[128,2048]{1,0:T(8,128)(2,1)S(1)} %collective-permute-done.8.refs_2_, ...), custom_call_target="tpu_custom_call" | custom-call | tf_op jit(solution)/shard_map/assemble/pallas_call | solution.py:200
  121.7 2.7 %scaled_step.1 = (bf16[2048,1024]{1,0:T(8,128)(2,1)}, f32[1,1024]{1,0:T(1,128)}) custom-call(f32[8,1024]{1,0:T(8,128)S(1)} %get-tuple-element.50.sums_ref, f32[1,1024]{1,0:T(1,128)S(1)} %bitcast.5, bf16[2048,1024]{1,0:T(8,128)(2,1)S(1)} %get-tuple-element.51.scaled_ref), custom_call_target="tpu_custom_call" | custom-call | tf_op jit(solution)/shard_map/scaled_step/pallas_call | solution.py:140
  (38 shorter events, 7.9 us)
Async XLA Ops:
  1.8 15.6 %collective-permute-start.7 = (bf16[128,1024]{1,0:T(8,128)(2,1)S(1)}, bf16[128,1024]{1,0:T(8,128)(2,1)S(1)}, u32[]{:S(2)}, u32[]{:S(2)}) collective-permute-start(bf16[128,1024]{1,0:T(8,128)(2,1)S(1)} %fusion.4.cot_ref), channel_id=1, source_target_pairs={{2,0},{3,1},{6,4},{7,5},{10,8},{11,9},{14,12},{15,13},{18,16},{19,... | collective-permute-start | bytes 786440 | tf_op jit(solution)/shard_map/ppermute | solution.py:28
  3.1 25.5 %collective-permute-start.9 = (bf16[128,1024]{1,0:T(8,128)(2,1)S(1)}, bf16[128,1024]{1,0:T(8,128)(2,1)S(1)}, u32[]{:S(2)}, u32[]{:S(2)}) collective-permute-start(bf16[128,1024]{1,0:T(8,128)(2,1)S(1)} %fusion.4.cot_ref), channel_id=1, source_target_pairs={{0,1},{1,2},{2,3},{4,5},{5,6},{6,7},{8,9},{9,10},{10,11},{12,13},{... | collective-permute-start | bytes 786440 | tf_op jit(solution)/shard_map/ppermute | solution.py:28
  6.4 22.4 %collective-permute-start.3 = (bf16[128,1024]{1,0:T(8,128)(2,1)S(1)}, bf16[128,1024]{1,0:T(8,128)(2,1)S(1)}, u32[]{:S(2)}, u32[]{:S(2)}) collective-permute-start(bf16[128,1024]{1,0:T(8,128)(2,1)S(1)} %fusion.4.cot_ref), channel_id=1, source_target_pairs={{0,2},{1,3},{4,6},{5,7},{8,10},{9,11},{12,14},{13,15},{16,18},{17,... | collective-permute-start | bytes 786440 | tf_op jit(solution)/shard_map/ppermute | solution.py:28
  11.3 29.1 %collective-permute-start.5 = (bf16[128,1024]{1,0:T(8,128)(2,1)S(1)}, bf16[128,1024]{1,0:T(8,128)(2,1)}, u32[]{:S(2)}, u32[]{:S(2)}) collective-permute-start(bf16[128,1024]{1,0:T(8,128)(2,1)S(1)} %fusion.4.cot_ref), channel_id=1, source_target_pairs={{1,0},{2,1},{3,2},{5,4},{6,5},{7,6},{9,8},{10,9},{11,10},{13,12},{... | collective-permute-start | bytes 786440 | tf_op jit(solution)/shard_map/ppermute | solution.py:28
  17.4 21.9 %collective-permute-start.10 = (bf16[128,1024]{1,0:T(8,128)(2,1)S(1)}, bf16[128,1024]{1,0:T(8,128)(2,1)}, u32[]{:S(2)}, u32[]{:S(2)}) collective-permute-start(bf16[128,1024]{1,0:T(8,128)(2,1)S(1)} %collective-permute-done.7), channel_id=1, source_target_pairs={{1,0},{5,4},{9,8},{13,12},{17,16},{21,20},{25,24},{29,28}} | collective-permute-start | bytes 786440 | tf_op jit(solution)/shard_map/ppermute | solution.py:39
  21.6 31.9 %collective-permute-start.12 = (bf16[128,2048]{1,0:T(8,128)(2,1)}, bf16[128,2048]{1,0:T(8,128)(2,1)S(1)}, u32[]{:S(2)}, u32[]{:S(2)}) collective-permute-start(bf16[128,2048]{1,0:T(8,128)(2,1)} %get-tuple-element.46), channel_id=1, source_target_pairs={{0,1},{1,2},{2,3},{3,0},{4,5},{5,6},{6,7},{7,4},{8,9},{9,10},{10,1... | collective-permute-start | bytes 1572872 | tf_op jit(solution)/shard_map/ppermute | solution.py:23
  24.4 2.2 %copy-start = (bf16[2048,1024]{1,0:T(8,128)(2,1)S(1)}, bf16[2048,1024]{1,0:T(8,128)(2,1)}, u32[]{:S(2)}) copy-start(bf16[2048,1024]{1,0:T(8,128)(2,1)} %weight_ref.7) | copy-start | bytes 12582916
  28.7 34.5 %collective-permute-start.13 = (bf16[128,2048]{1,0:T(8,128)(2,1)}, bf16[128,2048]{1,0:T(8,128)(2,1)S(1)}, u32[]{:S(2)}, u32[]{:S(2)}) collective-permute-start(bf16[128,2048]{1,0:T(8,128)(2,1)} %get-tuple-element.47), channel_id=1, source_target_pairs={{0,2},{1,3},{2,0},{3,1},{4,6},{5,7},{6,4},{7,5},{8,10},{9,11},{10,... | collective-permute-start | bytes 1572872 | tf_op jit(solution)/shard_map/ppermute | solution.py:23
  28.7 15.8 %collective-permute-start.4 = (bf16[128,1024]{1,0:T(8,128)(2,1)S(1)}, bf16[128,1024]{1,0:T(8,128)(2,1)S(1)}, u32[]{:S(2)}, u32[]{:S(2)}) collective-permute-start(bf16[128,1024]{1,0:T(8,128)(2,1)S(1)} %collective-permute-done.3), channel_id=1, source_target_pairs={{2,3},{6,7},{10,11},{14,15},{18,19},{22,23},{26,27},{30,31}} | collective-permute-start | bytes 786440 | tf_op jit(solution)/shard_map/ppermute | solution.py:39
  29.5 10.9 %copy-start.2 = (bf16[128,1024]{1,0:T(8,128)(2,1)}, bf16[128,1024]{1,0:T(8,128)(2,1)S(1)}, u32[]{:S(2)}) copy-start(bf16[128,1024]{1,0:T(8,128)(2,1)S(1)} %broadcast_select_fusion.1.cot_ref) | copy-start | bytes 786436
  39.4 58.7 %collective-permute-start.14 = (bf16[128,2048]{1,0:T(8,128)(2,1)}, bf16[128,2048]{1,0:T(8,128)(2,1)}, u32[]{:S(2)}, u32[]{:S(2)}) collective-permute-start(bf16[128,2048]{1,0:T(8,128)(2,1)} %get-tuple-element.48), channel_id=1, source_target_pairs={{0,3},{1,0},{2,1},{3,2},{4,7},{5,4},{6,5},{7,6},{8,11},{9,8},{10,9... | collective-permute-start | bytes 1572872 | tf_op jit(solution)/shard_map/ppermute | solution.py:23
  40.4 13.1 %copy-start.3 = (bf16[128,1024]{1,0:T(8,128)(2,1)}, bf16[128,1024]{1,0:T(8,128)(2,1)S(1)}, u32[]{:S(2)}) copy-start(bf16[128,1024]{1,0:T(8,128)(2,1)S(1)} %broadcast_select_fusion.cot_ref) | copy-start | bytes 786436
  40.4 78.2 %collective-permute-start.2 = (bf16[128,2048]{1,0:T(8,128)(2,1)S(1)}, bf16[128,2048]{1,0:T(8,128)(2,1)S(1)}, u32[]{:S(2)}, u32[]{:S(2)}) collective-permute-start(bf16[128,2048]{1,0:T(8,128)(2,1)S(1)} %lowered_block.4), channel_id=1, source_target_pairs={{4,0},{5,1},{6,2},{7,3},{8,4},{9,5},{10,6},{11,7},{12,8},{13,9},{1... | collective-permute-start | bytes 1572872 | tf_op jit(solution)/shard_map/ppermute | solution.py:60
  44.6 74.0 %collective-permute-start.8 = (bf16[128,2048]{1,0:T(8,128)(2,1)S(1)}, bf16[128,2048]{1,0:T(8,128)(2,1)S(1)}, u32[]{:S(2)}, u32[]{:S(2)}) collective-permute-start(bf16[128,2048]{1,0:T(8,128)(2,1)S(1)} %lowered_block.6), channel_id=1, source_target_pairs={{4,2},{5,3},{6,0},{7,1},{8,6},{9,7},{10,4},{11,5},{12,10},{13,11},... | collective-permute-start | bytes 1572872 | tf_op jit(solution)/shard_map/ppermute | solution.py:60
  47.9 5.6 %copy-start.4 = (bf16[128,1024]{1,0:T(8,128)(2,1)}, bf16[128,1024]{1,0:T(8,128)(2,1)S(1)}, u32[]{:S(2)}) copy-start(bf16[128,1024]{1,0:T(8,128)(2,1)S(1)} %broadcast_select_fusion.2.cot_ref) | copy-start | bytes 786436
  47.9 50.2 %copy-start.7 = (f32[2048]{0:T(1024)S(1)}, f32[2048]{0:T(1024)}, u32[]{:S(2)}) copy-start(f32[2048]{0:T(1024)} %param.12) | copy-start | bytes 24580
  53.5 65.1 %collective-permute-start.11 = (bf16[128,2048]{1,0:T(8,128)(2,1)}, bf16[128,2048]{1,0:T(8,128)(2,1)}, u32[]{:S(2)}, u32[]{:S(2)}) collective-permute-start(bf16[128,2048]{1,0:T(8,128)(2,1)} %lowered_block.7), channel_id=1, source_target_pairs={{4,3},{5,0},{6,1},{7,2},{8,7},{9,4},{10,5},{11,6},{12,11},{13,8},{... | collective-permute-start | bytes 1572872 | tf_op jit(solution)/shard_map/ppermute | solution.py:60
  63.1 55.5 %collective-permute-start.6 = (bf16[128,2048]{1,0:T(8,128)(2,1)}, bf16[128,2048]{1,0:T(8,128)(2,1)}, u32[]{:S(2)}, u32[]{:S(2)}) collective-permute-start(bf16[128,2048]{1,0:T(8,128)(2,1)} %lowered_block.5), channel_id=1, source_target_pairs={{4,1},{5,2},{6,3},{7,0},{8,5},{9,6},{10,7},{11,4},{12,9},{13,10},{... | collective-permute-start | bytes 1572872 | tf_op jit(solution)/shard_map/ppermute | solution.py:60
  98.1 0.8 copy-start.5
  98.1 1.0 copy-start.6
  105.3 3.4 %collective-permute-start = (f32[8,1024]{1,0:T(8,128)S(1)}, f32[8,1024]{1,0:T(8,128)S(1)}, u32[]{:S(2)}, u32[]{:S(2)}) collective-permute-start(f32[8,1024]{1,0:T(8,128)S(1)} %get-tuple-element.29), channel_id=1, source_target_pairs={{0,1},{1,0},{2,3},{3,2},{4,5},{5,4},{6,7},{7,6},{8,9},{9,8},{10,11... | collective-permute-start | bytes 98312 | tf_op jit(solution)/shard_map/cond/branch_1_fun/ppermute | solution.py:48
  108.7 9.9 %collective-permute-start.1 = (f32[8,1024]{1,0:T(8,128)S(1)}, f32[8,1024]{1,0:T(8,128)S(1)}, u32[]{:S(2)}, u32[]{:S(2)}) collective-permute-start(f32[8,1024]{1,0:T(8,128)S(1)} %add.21), channel_id=1, source_target_pairs={{0,2},{1,3},{2,0},{3,1},{4,6},{5,7},{6,4},{7,5},{8,10},{9,11},{10,... | collective-permute-start | bytes 98312 | tf_op jit(solution)/shard_map/cond/branch_1_fun/ppermute | solution.py:48
  118.6 3.1 %copy-start.1 = (f32[1024]{0:T(1024)S(1)}, f32[1024]{0:T(1024)}, u32[]{:S(2)}) copy-start(f32[1024]{0:T(1024)} %param.13) | copy-start | bytes 12292

commit v3 on v2

--- a/solution.py
+++ b/solution.py
@@ -18,25 +18,13 @@
     return lax.optimization_barrier((value, *others))[0]
 
 
-def ring(value, steps):
+def partner(steps, index, count):
+    return index ^ steps if count & (count - 1) == 0 else (steps - index) % count
+
+
+def trade(value, steps):
     count = lax.axis_size(DP)
-    return lax.ppermute(value, DP, [(i, (i + steps) % count) for i in range(count)])
-
-
-def reach(value, steps):
-    count = lax.axis_size(DP)
-    return lax.ppermute(
-        value, DP, [(i, i + steps) for i in range(count) if 0 <= i + steps < count]
-    )
-
-
-def hop(value, origin, steps):
-    count = lax.axis_size(DP)
-    if steps > 0:
-        pairs = [(i, i + 1) for i in range(origin, count - 1)]
-    else:
-        pairs = [(i, i - 1) for i in range(1, count - origin)]
-    return lax.ppermute(value, DP, pairs)
+    return lax.ppermute(value, DP, [(i, partner(steps, i, count)) for i in range(count)])
 
 
 def everyone(value):
@@ -53,7 +41,7 @@
 def hand_over(value, steps):
     count, sections = lax.axis_size(DP), lax.axis_size(SECTION)
     pairs = [
-        (s * count + i, (s - 1) * count + (i + steps) % count)
+        (s * count + i, (s - 1) * count + partner(steps, i, count))
         for s in range(1, sections)
         for i in range(count)
     ]
@@ -109,7 +97,7 @@
             pl.BlockSpec((8, units), lambda i: (0, 0)),
         ],
         out_shape=[
-            jax.ShapeDtypeStruct((rows, units), jnp.bfloat16),
+            jax.ShapeDtypeStruct((rows, units), jnp.float32),
             jax.ShapeDtypeStruct((1, rows), jnp.float32),
             jax.ShapeDtypeStruct((8, units), jnp.float32),
         ],
@@ -119,7 +107,10 @@
     )(*xs, *cs, row_state[:, None])
 
 
-def step_kernel(width, sums_ref, state_ref, scaled_ref, step_ref, col_ref, factor_ref):
+def finish_kernel(
+    width, count, me_ref, sums_ref, state_ref, scaled_ref, *refs
+):
+    parts, (step_ref, col_ref, upstream_ref, factor_ref) = refs[:count], refs[count:]
     units = scaled_ref.shape[1]
 
     @pl.when(pl.program_id(0) == 0)
@@ -131,33 +122,44 @@
         root_mean = jnp.sqrt(grand / (width * float(units)))
         factor_ref[...] = lax.rsqrt(col) * jnp.sqrt(average) / jnp.maximum(1.0, root_mean)
 
+    for k in range(count):
+        @pl.when(partner(k, me_ref[0], count) == pl.program_id(0))
+        def _(k=k):
+            upstream_ref[...] = parts[k][...]
+
     step_ref[...] = (scaled_ref[...] * factor_ref[...]).astype(step_ref.dtype)
 
 
-def step_call(scaled, sums, col_state, width, block=512):
+def finish(scaled, sums, col_state, width, parts, me):
+    count = len(parts)
     rows, units = scaled.shape
-    block = min(block, rows)
+    tokens = parts[0].shape[0]
+    block = rows // count
     return pl.pallas_call(
-        functools.partial(step_kernel, float(width)),
-        grid=(rows // block,),
+        functools.partial(finish_kernel, float(width), count),
+        grid=(count,),
         in_specs=[
+            pl.BlockSpec(memory_space=pltpu.SMEM),
             pl.BlockSpec((8, units), lambda i: (0, 0)),
             pl.BlockSpec((1, units), lambda i: (0, 0)),
             pl.BlockSpec((block, units), lambda i: (i, 0)),
-        ],
+        ]
+        + [pl.BlockSpec((tokens, rows), lambda i: (0, 0))] * count,
         out_specs=[
             pl.BlockSpec((block, units), lambda i: (i, 0)),
             pl.BlockSpec((1, units), lambda i: (0, 0)),
+            pl.BlockSpec((tokens, rows), lambda i: (0, i)),
         ],
         out_shape=[
             jax.ShapeDtypeStruct((rows, units), jnp.bfloat16),
             jax.ShapeDtypeStruct((1, units), jnp.float32),
+            jax.ShapeDtypeStruct((tokens, count * rows), parts[0].dtype),
         ],
         scratch_shapes=[pltpu.VMEM((1, units), jnp.float32)],
-        compiler_params=pltpu.CompilerParams(vmem_limit_bytes=16 * MIB),
+        compiler_params=pltpu.CompilerParams(vmem_limit_bytes=24 * MIB),
         cost_estimate=NO_COST,
-        name="scaled_step",
-    )(sums, col_state[None, :], scaled)
+        name="finish",
+    )(me[None], sums, col_state[None, :], scaled, *parts)
 
 
 def lowered_kernel(cot_ref, weight_ref, out_ref):
@@ -185,31 +187,6 @@
     )(cot, weight)
 
 
-def assemble_kernel(count, me_ref, *refs):
-    parts, out_ref = refs[:count], refs[count]
-    steps = lax.rem(me_ref[0] - pl.program_id(0) + count, count)
-    for k in range(count):
-        @pl.when(steps == k)
-        def _(k=k):
-            out_ref[...] = parts[k][...]
-
-
-def assemble(parts, me):
-    count = len(parts)
-    tokens, rows = parts[0].shape
-    return pl.pallas_call(
-        functools.partial(assemble_kernel, count),
-        grid=(count,),
-        in_specs=[pl.BlockSpec(memory_space=pltpu.SMEM)]
-        + [pl.BlockSpec((tokens, rows), lambda i: (0, 0))] * count,
-        out_specs=pl.BlockSpec((tokens, rows), lambda i: (0, i)),
-        out_shape=jax.ShapeDtypeStruct((tokens, count * rows), parts[0].dtype),
-        compiler_params=pltpu.CompilerParams(vmem_limit_bytes=16 * MIB),
-        cost_estimate=NO_COST,
-        name="assemble",
-    )(me[None], *parts)
-
-
 def local(inputs, hidden_grad, gate_pre, up_weight, row_state, col_state):
     count = lax.axis_size(DP)
     me = lax.axis_index(DP)
@@ -223,23 +200,32 @@
         hidden_grad.astype(jnp.float32) * jax.nn.silu(gate_pre.astype(jnp.float32))
     ).astype(jnp.bfloat16)
 
-    ahead = {1: reach(cotangent, 1), 2: reach(cotangent, 2)}
-    behind = {1: reach(cotangent, -1), 2: reach(cotangent, -2)}
-    for j in range(3, count):
-        ahead[j] = hop(ahead[j - 1], j - 1, 1)
-        behind[j] = hop(behind[j - 1], j - 1, -1)
-    cots = [cotangent] + [
-        jnp.where(me >= k, ahead[k], behind[count - k]) for k in range(1, count)
+    cots, xs = {0: cotangent}, {0: after(columns_of(me), cotangent)}
+    if count == 4:
+        inner, outward = [(1, 2), (2, 1)], [(1, 0), (2, 3)]
+        is_inner = (me == 1) | (me == 2)
+        cots[1] = trade(cotangent, 1)
+        middle = lax.ppermute(cotangent, DP, inner)
+        across = lax.ppermute(cots[1], DP, inner)
+        second = lax.ppermute(middle, DP, outward)
+        third = lax.ppermute(across, DP, outward)
+        cots[2] = jnp.where(is_inner, across, second)
+        cots[3] = jnp.where(is_inner, middle, third)
+        first, nearest = (across,), (third,)
+    else:
+        for k in range(1, count):
+            cots[k] = trade(cotangent, k)
+        first = nearest = (cots[1],)
+    for k in range(1, count):
+        xs[k] = trade(after(columns_of(partner(k, me, count)), *(first if k > 1 else nearest)), k)
+    cots = [cots[k] for k in range(count)]
+    xs = [xs[k] for k in range(count)]
+    low = [lowered(cots[k], up_weight) for k in range(count)]
+    waits = {3: (2, 3)}
+    sent = [
+        hand_over(after(low[k], *[xs[j] for j in waits.get(k, ())]) if k in waits else low[k], k)
+        for k in range(count)
     ]
-    order = list(range(1, count, 2)) + list(range(2, count, 2))
-    xs = {}
-    for k in order:
-        xs[k] = ring(after(columns_of(lax.rem(me + k, count)), cotangent), k)
-    xs[0] = after(columns_of(me), ahead[1])
-    xs = [xs[k] for k in range(count)]
-
-    low = [lowered(cots[(count - k) % count], up_weight) for k in range(count)]
-    sent = [hand_over(low[k], k) for k in range(count)]
 
     def update(xs, cots, row_state):
         scaled, row_new, sums = gradient_call(xs, cots, row_state)
@@ -247,7 +233,7 @@
 
     def nothing(xs, cots, row_state):
         return (
-            jnp.zeros((rows, units), jnp.bfloat16),
+            jnp.zeros((rows, units), jnp.float32),
             jnp.zeros((1, rows), jnp.float32),
             jnp.zeros((8, units), jnp.float32),
         )
@@ -255,8 +241,9 @@
     scaled, row_new, total = lax.cond(
         lax.optimization_barrier(me) < count, update, nothing, xs, cots, row_state
     )
-    upstream = assemble([sent[k] for k in range(count)], me)
-    step_out, col_new = step_call(scaled, after(total, upstream), col_state, width)
+    step_out, col_new, upstream = finish(
+        scaled, total, col_state, width, [sent[k] for k in range(count)], me
+    )
     return (upstream, step_out, row_new.reshape(-1), col_new.reshape(-1))
 
 

time: 127 us -> 117 us (0.921)
  starting transfers between devices: 68.5 us -> 44.7 us
  waiting for transfers between devices: 24 us -> 38.8 us
    ppermute x4, starting transfers between devices: 44.4 us -> 18.5 us  [hand_over(): return lax.ppermute(value, (SECTION, DP), pairs)]
    ppermute x9 -> x8, waiting for transfers between devices: 19.3 us -> 30.2 us  [the longest x4 30.2 us: trade(): lax.ppermute(value, DP, [(i, partner(steps, i, count)) for i in range(cou...]
    ppermute x2, starting transfers between devices: 8.62 us -> 14.1 us  [everyone(): lax.ppermute(value, DP, [(i, i ^ reach_of) for i in range(count)])]
    ppermute x2, waiting for transfers between devices: 4.67 us -> 8.59 us  [everyone(): lax.ppermute(value, DP, [(i, i ^ reach_of) for i in range(count)])]
    ppermute x9 -> x8, starting transfers between devices: 15.5 us -> 12.1 us  [the longest x4 7.53 us: trade(): lax.ppermute(value, DP, [(i, partner(steps, i, count)) for i in range(cou...]
    pallas_call x2 -> x1, Pallas kernels: 5.82 us -> 4.43 us  [finish(): pl.pallas_call(functools.partial(finish_kernel, float(width), count), gri...]
    select_n x3 -> x2, other arithmetic: 2 us -> 2.69 us  [the longest x1 1.7 us: local(): cots[3] = jnp.where(is_inner, middle, third)]
  transfers between devices with their start and end apart: 15 -> 14, of which waited for: 5 -> 5; matrix products, arithmetic and copies ran while one was open for 4% -> 5% of each run, Pallas kernels for 12% -> 14%
where the time goes in v3:
time: 117 us; the launch traced here: 115 us
  starting transfers between devices  44.7 us (38%)
  waiting for transfers between devices  38.8 us (33%)
  Pallas kernels  20.9 us (18%)
  local copies, waits for them, and re-layouts  6.25 us (5%)
  other arithmetic  3.9 us (3%)
    ppermute x4, waiting for transfers between devices, trade(): lax.ppermute(value, DP, [(i, partner(steps, i, count)) for i in range(cou...  30.2 us
    ppermute x4, starting transfers between devices, hand_over(): return lax.ppermute(value, (SECTION, DP), pairs)  18.5 us
    ppermute x2, starting transfers between devices, everyone(): lax.ppermute(value, DP, [(i, i ^ reach_of) for i in range(count)])  14.1 us
    pallas_call x4, Pallas kernels, lowered(): pl.pallas_call(lowered_kernel, grid=(rows // block,), in_specs=[pl.BlockS...  10.7 us
    ppermute x2, waiting for transfers between devices, everyone(): lax.ppermute(value, DP, [(i, i ^ reach_of) for i in range(count)])  8.59 us
    ppermute x4, starting transfers between devices, trade(): lax.ppermute(value, DP, [(i, partner(steps, i, count)) for i in range(cou...  7.53 us
    pallas_call x1, Pallas kernels, gradient_call(): pl.pallas_call(functools.partial(gradient_kernel, parts, min(256, block))...  5.77 us
    pallas_call x1, Pallas kernels, finish(): pl.pallas_call(functools.partial(finish_kernel, float(width), count), gri...  4.43 us
  transfers between devices with their start and end apart: 14, of which 5 were waited for; matrix products, arithmetic and copies ran while one was open for 5% of the time, Pallas kernels for 14%

profile of v3, /device:TPU:3, one launch (start us, length us, event | category | flops | bytes accessed | tf_op | source)
XLA Modules:
  0.0 115.5 jit_solution(8113396476983898513)
XLA Ops:
  1.8 1.4 %collective-permute-start.2 = (bf16[128,1024]{1,0:T(8,128)(2,1)S(1)}, bf16[128,1024]{1,0:T(8,128)(2,1)S(1)}, u32[]{:S(2)}, u32[]{:S(2)}) collective-permute-start(bf16[128,1024]{1,0:T(8,128)(2,1)S(1)} %fusion.4.cot_ref), channel_id=1, source_target_pairs={{0,1},{1,0},{2,3},{3,2},{4,5},{5,4},{6,7},{7,6},{8,9},{9,8},{10,11... | collective-permute-start | bytes 786440 | tf_op jit(solution)/shard_map/ppermute | solution.py:27
  3.9 5.2 %collective-permute-done.2.cot_ref = bf16[128,1024]{1,0:T(8,128)(2,1)S(1)} collective-permute-done((bf16[128,1024]{1,0:T(8,128)(2,1)S(1)}, bf16[128,1024]{1,0:T(8,128)(2,1)S(1)}, u32[]{:S(2)}, u32[]{:S(2)}) %collective-permute-start.2) | collective-permute-done | bytes 262176 | tf_op jit(solution)/shard_map/ppermute | solution.py:27
  9.1 1.4 %collective-permute-start.3 = (bf16[128,1024]{1,0:T(8,128)(2,1)S(1)}, bf16[128,1024]{1,0:T(8,128)(2,1)}, u32[]{:S(2)}, u32[]{:S(2)}) collective-permute-start(bf16[128,1024]{1,0:T(8,128)(2,1)S(1)} %collective-permute-done.2.cot_ref), channel_id=1, source_target_pairs={{1,2},{2,1},{5,6},{6,5},{9,10},{10,9},{13,14},{14,13},{17,18},{18,... | collective-permute-start | bytes 786440 | tf_op jit(solution)/shard_map/ppermute | solution.py:209
  11.7 2.9 %constant_dynamic-slice_fusion = (bf16[128,2048]{1,0:T(8,128)(2,1)}, bf16[128,2048]{1,0:T(8,128)(2,1)}, bf16[128,2048]{1,0:T(8,128)(2,1)}, bf16[128,2048]{1,0:T(8,128)(2,1)}) fusion(bf16[128,8192]{1,0:T(8,128)(2,1)} %param.8, s32[]{:T(128)S(6)} %select_n.27, s32[]{:T(128)S(6)} %select_n.25, s32[]{:T(128)S(6)} %select_n.24, s32[]{:T(128)S(6)} %select_n.26), kind=kLoop, calls=%fused_computation.9 | loop fusion | bytes 4194320 | tf_op jit(solution)/shard_map/dynamic_slice | solution.py:197
  14.6 5.0 %collective-permute-start.6 = (bf16[128,2048]{1,0:T(8,128)(2,1)}, bf16[128,2048]{1,0:T(8,128)(2,1)S(1)}, u32[]{:S(2)}, u32[]{:S(2)}) collective-permute-start(bf16[128,2048]{1,0:T(8,128)(2,1)} %get-tuple-element.48), channel_id=1, source_target_pairs={{0,2},{1,3},{2,0},{3,1},{4,6},{5,7},{6,4},{7,5},{8,10},{9,11},{10,... | collective-permute-start | bytes 1572872 | tf_op jit(solution)/shard_map/ppermute | solution.py:27
  22.0 2.0 %lowered_block.4 = bf16[128,2048]{1,0:T(8,128)(2,1)S(1)} custom-call(bf16[128,1024]{1,0:T(8,128)(2,1)S(1)} %fusion.4.cot_ref, bf16[2048,1024]{1,0:T(8,128)(2,1)S(1)} %copy-done), custom_call_target="tpu_custom_call" | custom-call | tf_op jit(solution)/shard_map/lowered_block/pallas_call | solution.py:175
  24.0 4.9 %collective-permute-start.10 = (bf16[128,2048]{1,0:T(8,128)(2,1)S(1)}, bf16[128,2048]{1,0:T(8,128)(2,1)S(1)}, u32[]{:S(2)}, u32[]{:S(2)}) collective-permute-start(bf16[128,2048]{1,0:T(8,128)(2,1)S(1)} %lowered_block.4), channel_id=1, source_target_pairs={{4,0},{5,1},{6,2},{7,3},{8,4},{9,5},{10,6},{11,7},{12,8},{13,9},{1... | collective-permute-start | bytes 1572872 | tf_op jit(solution)/shard_map/ppermute | solution.py:48
  29.0 2.2 %copy-done.1 = bf16[2048,1024]{1,0:T(8,128)(2,1)S(1)} copy-done((bf16[2048,1024]{1,0:T(8,128)(2,1)S(1)}, bf16[2048,1024]{1,0:T(8,128)(2,1)}, u32[]{:S(2)}) %copy-start.1) | copy-done | bytes 4194328
  31.2 2.0 %lowered_block.5 = bf16[128,2048]{1,0:T(8,128)(2,1)S(1)} custom-call(bf16[128,1024]{1,0:T(8,128)(2,1)S(1)} %collective-permute-done.2.cot_ref, bf16[2048,1024]{1,0:T(8,128)(2,1)S(1)} %copy-done.1), custom_call_target="tpu_custom_call" | custom-call | tf_op jit(solution)/shard_map/lowered_block/pallas_call | solution.py:175
  33.2 4.9 %collective-permute-start.11 = (bf16[128,2048]{1,0:T(8,128)(2,1)S(1)}, bf16[128,2048]{1,0:T(8,128)(2,1)S(1)}, u32[]{:S(2)}, u32[]{:S(2)}) collective-permute-start(bf16[128,2048]{1,0:T(8,128)(2,1)S(1)} %lowered_block.5), channel_id=1, source_target_pairs={{4,1},{5,0},{6,3},{7,2},{8,5},{9,4},{10,7},{11,6},{12,9},{13,8},{1... | collective-permute-start | bytes 1572872 | tf_op jit(solution)/shard_map/ppermute | solution.py:48
  39.1 2.9 %lowered_block.6 = bf16[128,2048]{1,0:T(8,128)(2,1)} custom-call(bf16[128,1024]{1,0:T(8,128)(2,1)S(1)} %broadcast_select_fusion.1.cot_ref, bf16[2048,1024]{1,0:T(8,128)(2,1)S(1)} %copy-done.1), custom_call_target="tpu_custom_call" | custom-call | tf_op jit(solution)/shard_map/lowered_block/pallas_call | solution.py:175
  42.1 1.7 %broadcast_select_fusion.cot_ref = bf16[128,1024]{1,0:T(8,128)(2,1)} fusion(bf16[128,1024]{1,0:T(8,128)(2,1)S(1)} %collective-permute-done.8, bf16[128,1024]{1,0:T(8,128)(2,1)} %collective-permute-done.4, pred[]{:T(512)S(6)} %or.3), kind=kLoop, calls=%fused_computation.7 | loop fusion | flops 131072 | bytes 786433 | tf_op jit(solution)/shard_map/jit(_where)/select_n | solution.py:213
  43.8 3.8 %lowered_block.7 = bf16[128,2048]{1,0:T(8,128)(2,1)} custom-call(bf16[128,1024]{1,0:T(8,128)(2,1)} %broadcast_select_fusion.cot_ref, bf16[2048,1024]{1,0:T(8,128)(2,1)S(1)} %copy-done.1), custom_call_target="tpu_custom_call" | custom-call | tf_op jit(solution)/shard_map/lowered_block/pallas_call | solution.py:175
  47.6 6.1 %collective-permute-done.6 = bf16[128,2048]{1,0:T(8,128)(2,1)S(1)} collective-permute-done((bf16[128,2048]{1,0:T(8,128)(2,1)}, bf16[128,2048]{1,0:T(8,128)(2,1)S(1)}, u32[]{:S(2)}, u32[]{:S(2)}) %collective-permute-start.6) | collective-permute-done | bytes 524320 | tf_op jit(solution)/shard_map/ppermute | solution.py:27
  53.7 3.9 %collective-permute-start.12 = (bf16[128,2048]{1,0:T(8,128)(2,1)}, bf16[128,2048]{1,0:T(8,128)(2,1)}, u32[]{:S(2)}, u32[]{:S(2)}) collective-permute-start(bf16[128,2048]{1,0:T(8,128)(2,1)} %lowered_block.6), channel_id=1, source_target_pairs={{4,2},{5,3},{6,0},{7,1},{8,6},{9,7},{10,4},{11,5},{12,10},{13,11},... | collective-permute-start | bytes 1572872 | tf_op jit(solution)/shard_map/ppermute | solution.py:48
  57.6 4.7 %collective-permute-start.13 = (bf16[128,2048]{1,0:T(8,128)(2,1)}, bf16[128,2048]{1,0:T(8,128)(2,1)}, u32[]{:S(2)}, u32[]{:S(2)}) collective-permute-start(bf16[128,2048]{1,0:T(8,128)(2,1)} %lowered_block.7), channel_id=1, source_target_pairs={{4,3},{5,2},{6,1},{7,0},{8,7},{9,6},{10,5},{11,4},{12,11},{13,10},... | collective-permute-start | bytes 1572872 | tf_op jit(solution)/shard_map/ppermute | solution.py:48
  62.4 18.9 %collective-permute-done.5 = bf16[128,2048]{1,0:T(8,128)(2,1)} collective-permute-done((bf16[128,2048]{1,0:T(8,128)(2,1)}, bf16[128,2048]{1,0:T(8,128)(2,1)}, u32[]{:S(2)}, u32[]{:S(2)}) %collective-permute-start.5) | collective-permute-done | bytes 524320 | tf_op jit(solution)/shard_map/ppermute | solution.py:27
  81.3 29.6 %conditional.1 = (f32[2048,1024]{1,0:T(8,128)S(1)}, f32[8,1024]{1,0:T(8,128)S(1)}, f32[2048]{0:T(1024)}) conditional(s32[]{:T(128)} %convert_element_type.12, () %tuple.23, (f32[2048]{0:T(1024)S(1)}, bf16[128,2048]{1,0:T(8,128)(2,1)}, bf16[128,2048]{1,0:T(8,128)(2,1)}, bf16[128,2048]{1,0:T(8,128)(2,1)S(1)}, bf16[128,2048]{1,0:T(8,128)(2,1)}, ...), branch_computations={%region_0.1_spmd, %region_1.2_spmd} | conditional | flops 16384 | bytes 8429604 | solution.py:241
  82.5 5.8 %gradient_and_sums.1 = (f32[2048,1024]{1,0:T(8,128)S(1)}, f32[1,2048]{1,0:T(1,128)}, f32[8,1024]{1,0:T(8,128)S(1)}) custom-call(bf16[128,2048]{1,0:T(8,128)(2,1)} %get-tuple-element.19.refs_0_, bf16[128,2048]{1,0:T(8,128)(2,1)} %get-tuple-element.20.refs_1_, bf16[128,2048]{1,0:T(8,128)(2,1)} %copy-done.5, bf16[128,2048]{1,0:T(8,128)(2,1)} %get-tuple-element.22.refs_3_, ...), custom_call_target="tpu_custom_call" | custom-call | tf_op jit(solution)/shard_map/cond/branch_1_fun/gradient_and_sums/pallas_call | solution.py:88
  88.3 12.4 %collective-permute-start = (f32[8,1024]{1,0:T(8,128)S(1)}, f32[8,1024]{1,0:T(8,128)S(1)}, u32[]{:S(2)}, u32[]{:S(2)}) collective-permute-start(f32[8,1024]{1,0:T(8,128)S(1)} %get-tuple-element.29), channel_id=1, source_target_pairs={{0,1},{1,0},{2,3},{3,2},{4,5},{5,4},{6,7},{7,6},{8,9},{9,8},{10,11... | collective-permute-start | bytes 98312 | tf_op jit(solution)/shard_map/cond/branch_1_fun/ppermute | solution.py:36
  100.6 1.3 %collective-permute-done = f32[8,1024]{1,0:T(8,128)S(1)} collective-permute-done((f32[8,1024]{1,0:T(8,128)S(1)}, f32[8,1024]{1,0:T(8,128)S(1)}, u32[]{:S(2)}, u32[]{:S(2)}) %collective-permute-start) | collective-permute-done | bytes 32800 | tf_op jit(solution)/shard_map/cond/branch_1_fun/ppermute | solution.py:36
  101.9 1.8 %collective-permute-start.1 = (f32[8,1024]{1,0:T(8,128)S(1)}, f32[8,1024]{1,0:T(8,128)S(1)}, u32[]{:S(2)}, u32[]{:S(2)}) collective-permute-start(f32[8,1024]{1,0:T(8,128)S(1)} %add.15), channel_id=1, source_target_pairs={{0,2},{1,3},{2,0},{3,1},{4,6},{5,7},{6,4},{7,5},{8,10},{9,11},{10,... | collective-permute-start | bytes 98312 | tf_op jit(solution)/shard_map/cond/branch_1_fun/ppermute | solution.py:36
  103.7 7.3 %collective-permute-done.1 = f32[8,1024]{1,0:T(8,128)S(1)} collective-permute-done((f32[8,1024]{1,0:T(8,128)S(1)}, f32[8,1024]{1,0:T(8,128)S(1)}, u32[]{:S(2)}, u32[]{:S(2)}) %collective-permute-start.1) | collective-permute-done | bytes 32800 | tf_op jit(solution)/shard_map/cond/branch_1_fun/ppermute | solution.py:36
  111.0 4.4 %finish.1 = (bf16[2048,1024]{1,0:T(8,128)(2,1)}, f32[1,1024]{1,0:T(1,128)}, bf16[128,8192]{1,0:T(8,128)(2,1)}) custom-call(s32[1]{0:T(128)} %bitcast.2.me_ref, f32[8,1024]{1,0:T(8,128)S(1)} %get-tuple-element.50.sums_ref, f32[1,1024]{1,0:T(1,128)S(1)} %bitcast.5, f32[2048,1024]{1,0:T(8,128)S(1)} %get-tuple-element.51.scaled_ref, ...), custom_call_target="tpu_custom_call" | custom-call | tf_op jit(solution)/shard_map/finish/pallas_call | solution.py:138
  (32 shorter events, 7.8 us)
Async XLA Ops:
  1.8 7.2 %collective-permute-start.2 = (bf16[128,1024]{1,0:T(8,128)(2,1)S(1)}, bf16[128,1024]{1,0:T(8,128)(2,1)S(1)}, u32[]{:S(2)}, u32[]{:S(2)}) collective-permute-start(bf16[128,1024]{1,0:T(8,128)(2,1)S(1)} %fusion.4.cot_ref), channel_id=1, source_target_pairs={{0,1},{1,0},{2,3},{3,2},{4,5},{5,4},{6,7},{7,6},{8,9},{9,8},{10,11... | collective-permute-start | bytes 786440 | tf_op jit(solution)/shard_map/ppermute | solution.py:27
  3.2 7.2 %collective-permute-start.8 = (bf16[128,1024]{1,0:T(8,128)(2,1)S(1)}, bf16[128,1024]{1,0:T(8,128)(2,1)S(1)}, u32[]{:S(2)}, u32[]{:S(2)}) collective-permute-start(bf16[128,1024]{1,0:T(8,128)(2,1)S(1)} %fusion.4.cot_ref), channel_id=1, source_target_pairs={{1,2},{2,1},{5,6},{6,5},{9,10},{10,9},{13,14},{14,13},{17,18},{18,... | collective-permute-start | bytes 786440 | tf_op jit(solution)/shard_map/ppermute | solution.py:208
  3.9 18.1 %copy-start = (bf16[2048,1024]{1,0:T(8,128)(2,1)S(1)}, bf16[2048,1024]{1,0:T(8,128)(2,1)}, u32[]{:S(2)}) copy-start(bf16[2048,1024]{1,0:T(8,128)(2,1)} %weight_ref.7) | copy-start | bytes 12582916
  9.1 19.9 %copy-start.4 = (bf16[128,1024]{1,0:T(8,128)(2,1)}, bf16[128,1024]{1,0:T(8,128)(2,1)S(1)}, u32[]{:S(2)}) copy-start(bf16[128,1024]{1,0:T(8,128)(2,1)S(1)} %collective-permute-done.2.cot_ref) | copy-start | bytes 786436
  9.1 5.5 %collective-permute-start.3 = (bf16[128,1024]{1,0:T(8,128)(2,1)S(1)}, bf16[128,1024]{1,0:T(8,128)(2,1)}, u32[]{:S(2)}, u32[]{:S(2)}) collective-permute-start(bf16[128,1024]{1,0:T(8,128)(2,1)S(1)} %collective-permute-done.2.cot_ref), channel_id=1, source_target_pairs={{1,2},{2,1},{5,6},{6,5},{9,10},{10,9},{13,14},{14,13},{17,18},{18,... | collective-permute-start | bytes 786440 | tf_op jit(solution)/shard_map/ppermute | solution.py:209
  10.4 22.8 %collective-permute-start.9 = (bf16[128,1024]{1,0:T(8,128)(2,1)S(1)}, bf16[128,1024]{1,0:T(8,128)(2,1)}, u32[]{:S(2)}, u32[]{:S(2)}) collective-permute-start(bf16[128,1024]{1,0:T(8,128)(2,1)S(1)} %collective-permute-done.8), channel_id=1, source_target_pairs={{1,0},{2,3},{5,4},{6,7},{9,8},{10,11},{13,12},{14,15},{17,16},{18,... | collective-permute-start | bytes 786440 | tf_op jit(solution)/shard_map/ppermute | solution.py:210
  14.6 39.1 %collective-permute-start.6 = (bf16[128,2048]{1,0:T(8,128)(2,1)}, bf16[128,2048]{1,0:T(8,128)(2,1)S(1)}, u32[]{:S(2)}, u32[]{:S(2)}) collective-permute-start(bf16[128,2048]{1,0:T(8,128)(2,1)} %get-tuple-element.48), channel_id=1, source_target_pairs={{0,2},{1,3},{2,0},{3,1},{4,6},{5,7},{6,4},{7,5},{8,10},{9,11},{10,... | collective-permute-start | bytes 1572872 | tf_op jit(solution)/shard_map/ppermute | solution.py:27
  19.6 38.0 %collective-permute-start.7 = (bf16[128,2048]{1,0:T(8,128)(2,1)}, bf16[128,2048]{1,0:T(8,128)(2,1)}, u32[]{:S(2)}, u32[]{:S(2)}) collective-permute-start(bf16[128,2048]{1,0:T(8,128)(2,1)} %get-tuple-element.49), channel_id=1, source_target_pairs={{0,3},{1,2},{2,1},{3,0},{4,7},{5,6},{6,5},{7,4},{8,11},{9,10},{10,... | collective-permute-start | bytes 1572872 | tf_op jit(solution)/shard_map/ppermute | solution.py:27
  20.7 21.3 %collective-permute-start.4 = (bf16[128,1024]{1,0:T(8,128)(2,1)}, bf16[128,1024]{1,0:T(8,128)(2,1)}, u32[]{:S(2)}, u32[]{:S(2)}) collective-permute-start(bf16[128,1024]{1,0:T(8,128)(2,1)} %collective-permute-done.3), channel_id=1, source_target_pairs={{1,0},{2,3},{5,4},{6,7},{9,8},{10,11},{13,12},{14,15},{17,16},{18,... | collective-permute-start | bytes 786440 | tf_op jit(solution)/shard_map/ppermute | solution.py:211
  24.0 86.9 %collective-permute-start.10 = (bf16[128,2048]{1,0:T(8,128)(2,1)S(1)}, bf16[128,2048]{1,0:T(8,128)(2,1)S(1)}, u32[]{:S(2)}, u32[]{:S(2)}) collective-permute-start(bf16[128,2048]{1,0:T(8,128)(2,1)S(1)} %lowered_block.4), channel_id=1, source_target_pairs={{4,0},{5,1},{6,2},{7,3},{8,4},{9,5},{10,6},{11,7},{12,8},{13,9},{1... | collective-permute-start | bytes 1572872 | tf_op jit(solution)/shard_map/ppermute | solution.py:48
  29.0 2.2 %copy-start.1 = (bf16[2048,1024]{1,0:T(8,128)(2,1)S(1)}, bf16[2048,1024]{1,0:T(8,128)(2,1)}, u32[]{:S(2)}) copy-start(bf16[2048,1024]{1,0:T(8,128)(2,1)} %weight_ref.7) | copy-start | bytes 12582916
  33.2 77.8 %collective-permute-start.11 = (bf16[128,2048]{1,0:T(8,128)(2,1)S(1)}, bf16[128,2048]{1,0:T(8,128)(2,1)S(1)}, u32[]{:S(2)}, u32[]{:S(2)}) collective-permute-start(bf16[128,2048]{1,0:T(8,128)(2,1)S(1)} %lowered_block.5), channel_id=1, source_target_pairs={{4,1},{5,0},{6,3},{7,2},{8,5},{9,4},{10,7},{11,6},{12,9},{13,8},{1... | collective-permute-start | bytes 1572872 | tf_op jit(solution)/shard_map/ppermute | solution.py:48
  39.1 42.2 %copy-start.3 = (bf16[128,1024]{1,0:T(8,128)(2,1)}, bf16[128,1024]{1,0:T(8,128)(2,1)S(1)}, u32[]{:S(2)}) copy-start(bf16[128,1024]{1,0:T(8,128)(2,1)S(1)} %broadcast_select_fusion.1.cot_ref) | copy-start | bytes 786436
  39.1 42.2 %copy-start.6 = (f32[2048]{0:T(1024)S(1)}, f32[2048]{0:T(1024)}, u32[]{:S(2)}) copy-start(f32[2048]{0:T(1024)} %param.12) | copy-start | bytes 24580
  42.0 39.3 %collective-permute-start.5 = (bf16[128,2048]{1,0:T(8,128)(2,1)}, bf16[128,2048]{1,0:T(8,128)(2,1)}, u32[]{:S(2)}, u32[]{:S(2)}) collective-permute-start(bf16[128,2048]{1,0:T(8,128)(2,1)} %get-tuple-element.47), channel_id=1, source_target_pairs={{0,1},{1,0},{2,3},{3,2},{4,5},{5,4},{6,7},{7,6},{8,9},{9,8},{10,11... | collective-permute-start | bytes 1572872 | tf_op jit(solution)/shard_map/ppermute | solution.py:27
  53.7 57.3 %collective-permute-start.12 = (bf16[128,2048]{1,0:T(8,128)(2,1)}, bf16[128,2048]{1,0:T(8,128)(2,1)}, u32[]{:S(2)}, u32[]{:S(2)}) collective-permute-start(bf16[128,2048]{1,0:T(8,128)(2,1)} %lowered_block.6), channel_id=1, source_target_pairs={{4,2},{5,3},{6,0},{7,1},{8,6},{9,7},{10,4},{11,5},{12,10},{13,11},... | collective-permute-start | bytes 1572872 | tf_op jit(solution)/shard_map/ppermute | solution.py:48
  57.6 53.4 %collective-permute-start.13 = (bf16[128,2048]{1,0:T(8,128)(2,1)}, bf16[128,2048]{1,0:T(8,128)(2,1)}, u32[]{:S(2)}, u32[]{:S(2)}) collective-permute-start(bf16[128,2048]{1,0:T(8,128)(2,1)} %lowered_block.7), channel_id=1, source_target_pairs={{4,3},{5,2},{6,1},{7,0},{8,7},{9,6},{10,5},{11,4},{12,11},{13,10},... | collective-permute-start | bytes 1572872 | tf_op jit(solution)/shard_map/ppermute | solution.py:48
  81.3 29.7 %copy-start.2 = (f32[1024]{0:T(1024)S(1)}, f32[1024]{0:T(1024)}, u32[]{:S(2)}) copy-start(f32[1024]{0:T(1024)} %param.13) | copy-start | bytes 12292
  81.3 0.8 copy-start.5
  88.3 13.7 %collective-permute-start = (f32[8,1024]{1,0:T(8,128)S(1)}, f32[8,1024]{1,0:T(8,128)S(1)}, u32[]{:S(2)}, u32[]{:S(2)}) collective-permute-start(f32[8,1024]{1,0:T(8,128)S(1)} %get-tuple-element.29), channel_id=1, source_target_pairs={{0,1},{1,0},{2,3},{3,2},{4,5},{5,4},{6,7},{7,6},{8,9},{9,8},{10,11... | collective-permute-start | bytes 98312 | tf_op jit(solution)/shard_map/cond/branch_1_fun/ppermute | solution.py:36
  101.9 9.0 %collective-permute-start.1 = (f32[8,1024]{1,0:T(8,128)S(1)}, f32[8,1024]{1,0:T(8,128)S(1)}, u32[]{:S(2)}, u32[]{:S(2)}) collective-permute-start(f32[8,1024]{1,0:T(8,128)S(1)} %add.15), channel_id=1, source_target_pairs={{0,2},{1,3},{2,0},{3,1},{4,6},{5,7},{6,4},{7,5},{8,10},{9,11},{10,... | collective-permute-start | bytes 98312 | tf_op jit(solution)/shard_map/cond/branch_1_fun/ppermute | solution.py:36

commit v4 on v3

--- a/solution.py
+++ b/solution.py
@@ -104,7 +104,7 @@
         compiler_params=pltpu.CompilerParams(vmem_limit_bytes=24 * MIB),
         cost_estimate=NO_COST,
         name="gradient_and_sums",
-    )(*xs, *cs, row_state[:, None])
+    )(*xs, *cs, row_state)
 
 
 def finish_kernel(
@@ -200,6 +200,7 @@
         hidden_grad.astype(jnp.float32) * jax.nn.silu(gate_pre.astype(jnp.float32))
     ).astype(jnp.bfloat16)
 
+    row_state = after(row_state[:, None], cotangent)
     cots, xs = {0: cotangent}, {0: after(columns_of(me), cotangent)}
     if count == 4:
         inner, outward = [(1, 2), (2, 1)], [(1, 0), (2, 3)]
@@ -221,7 +222,7 @@
     cots = [cots[k] for k in range(count)]
     xs = [xs[k] for k in range(count)]
     low = [lowered(cots[k], up_weight) for k in range(count)]
-    waits = {3: (2, 3)}
+    waits = {0: (2,), 3: (2, 3)}
     sent = [
         hand_over(after(low[k], *[xs[j] for j in waits.get(k, ())]) if k in waits else low[k], k)
         for k in range(count)

time: 117 us -> 117 us (level)
  waiting for transfers between devices: 38.8 us -> 34.9 us
  starting transfers between devices: 44.7 us -> 47.4 us
  local copies, waits for them, and re-layouts: 6.25 us -> 8.43 us
    ppermute x4, waiting for transfers between devices: 30.2 us -> 18.4 us  [trade(): lax.ppermute(value, DP, [(i, partner(steps, i, count)) for i in range(cou...]
    ppermute x4, starting transfers between devices: 18.5 us -> 28.5 us  [hand_over(): return lax.ppermute(value, (SECTION, DP), pairs)]
    ppermute x2, waiting for transfers between devices: 8.59 us -> 16.4 us  [everyone(): lax.ppermute(value, DP, [(i, i ^ reach_of) for i in range(count)])]
    ppermute x2, starting transfers between devices: 14.1 us -> 6.89 us  [everyone(): lax.ppermute(value, DP, [(i, i ^ reach_of) for i in range(count)])]
    unnamed x12, local copies, waits for them, and re-layouts: 2.21 us -> 4.38 us
  transfers between devices with their start and end apart: 14 -> 14, of which waited for: 5 -> 5; matrix products, arithmetic and copies ran while one was open for 5% -> 4% of each run, Pallas kernels for 14% -> 14%
where the time goes in v4:
time: 117 us; the launch traced here: 115 us
  starting transfers between devices  47.4 us (41%)
  waiting for transfers between devices  34.9 us (30%)
  Pallas kernels  20.9 us (18%)
  local copies, waits for them, and re-layouts  8.43 us (7%)
  other arithmetic  2.96 us (3%)
    ppermute x4, starting transfers between devices, hand_over(): return lax.ppermute(value, (SECTION, DP), pairs)  28.5 us
    ppermute x4, waiting for transfers between devices, trade(): lax.ppermute(value, DP, [(i, partner(steps, i, count)) for i in range(cou...  18.4 us
    ppermute x2, waiting for transfers between devices, everyone(): lax.ppermute(value, DP, [(i, i ^ reach_of) for i in range(count)])  16.4 us
    pallas_call x4, Pallas kernels, lowered(): pl.pallas_call(lowered_kernel, grid=(rows // block,), in_specs=[pl.BlockS...  10.7 us
    ppermute x4, starting transfers between devices, trade(): lax.ppermute(value, DP, [(i, partner(steps, i, count)) for i in range(cou...  7.5 us
    ppermute x2, starting transfers between devices, everyone(): lax.ppermute(value, DP, [(i, i ^ reach_of) for i in range(count)])  6.89 us
    pallas_call x1, Pallas kernels, gradient_call(): pl.pallas_call(functools.partial(gradient_kernel, parts, min(256, block))...  5.77 us
    pallas_call x1, Pallas kernels, finish(): pl.pallas_call(functools.partial(finish_kernel, float(width), count), gri...  4.43 us
  transfers between devices with their start and end apart: 14, of which 5 were waited for; matrix products, arithmetic and copies ran while one was open for 4% of the time, Pallas kernels for 14%

profile of v4, /device:TPU:3, one launch (start us, length us, event | category | flops | bytes accessed | tf_op | source)
XLA Modules:
  0.0 115.5 jit_solution(136263782813760087)
XLA Ops:
  1.8 1.4 %collective-permute-start.2 = (bf16[128,1024]{1,0:T(8,128)(2,1)S(1)}, bf16[128,1024]{1,0:T(8,128)(2,1)S(1)}, u32[]{:S(2)}, u32[]{:S(2)}) collective-permute-start(bf16[128,1024]{1,0:T(8,128)(2,1)S(1)} %fusion.4.cot_ref), channel_id=1, source_target_pairs={{0,1},{1,0},{2,3},{3,2},{4,5},{5,4},{6,7},{7,6},{8,9},{9,8},{10,11... | collective-permute-start | bytes 786440 | tf_op jit(solution)/shard_map/ppermute | solution.py:27
  3.9 5.2 %collective-permute-done.2.cot_ref = bf16[128,1024]{1,0:T(8,128)(2,1)S(1)} collective-permute-done((bf16[128,1024]{1,0:T(8,128)(2,1)S(1)}, bf16[128,1024]{1,0:T(8,128)(2,1)S(1)}, u32[]{:S(2)}, u32[]{:S(2)}) %collective-permute-start.2) | collective-permute-done | bytes 262176 | tf_op jit(solution)/shard_map/ppermute | solution.py:27
  9.1 1.4 %collective-permute-start.3 = (bf16[128,1024]{1,0:T(8,128)(2,1)S(1)}, bf16[128,1024]{1,0:T(8,128)(2,1)}, u32[]{:S(2)}, u32[]{:S(2)}) collective-permute-start(bf16[128,1024]{1,0:T(8,128)(2,1)S(1)} %collective-permute-done.2.cot_ref), channel_id=1, source_target_pairs={{1,2},{2,1},{5,6},{6,5},{9,10},{10,9},{13,14},{14,13},{17,18},{18,... | collective-permute-start | bytes 786440 | tf_op jit(solution)/shard_map/ppermute | solution.py:210
  11.7 2.9 %constant_dynamic-slice_fusion = (bf16[128,2048]{1,0:T(8,128)(2,1)}, bf16[128,2048]{1,0:T(8,128)(2,1)}, bf16[128,2048]{1,0:T(8,128)(2,1)}, bf16[128,2048]{1,0:T(8,128)(2,1)}) fusion(bf16[128,8192]{1,0:T(8,128)(2,1)} %param.8, s32[]{:T(128)S(6)} %select_n.27, s32[]{:T(128)S(6)} %select_n.25, s32[]{:T(128)S(6)} %select_n.24, s32[]{:T(128)S(6)} %select_n.26), kind=kLoop, calls=%fused_computation.9 | loop fusion | bytes 4194320 | tf_op jit(solution)/shard_map/dynamic_slice | solution.py:197
  14.6 5.0 %collective-permute-start.6 = (bf16[128,2048]{1,0:T(8,128)(2,1)}, bf16[128,2048]{1,0:T(8,128)(2,1)S(1)}, u32[]{:S(2)}, u32[]{:S(2)}) collective-permute-start(bf16[128,2048]{1,0:T(8,128)(2,1)} %get-tuple-element.50), channel_id=1, source_target_pairs={{0,2},{1,3},{2,0},{3,1},{4,6},{5,7},{6,4},{7,5},{8,10},{9,11},{10,... | collective-permute-start | bytes 1572872 | tf_op jit(solution)/shard_map/ppermute | solution.py:27
  22.0 2.2 %copy-done = bf16[2048,1024]{1,0:T(8,128)(2,1)S(1)} copy-done((bf16[2048,1024]{1,0:T(8,128)(2,1)S(1)}, bf16[2048,1024]{1,0:T(8,128)(2,1)}, u32[]{:S(2)}) %copy-start) | copy-done | bytes 4194328
  24.2 2.1 %lowered_block.4 = bf16[128,2048]{1,0:T(8,128)(2,1)S(1)} custom-call(bf16[128,1024]{1,0:T(8,128)(2,1)S(1)} %fusion.4.cot_ref, bf16[2048,1024]{1,0:T(8,128)(2,1)S(1)} %copy-done), custom_call_target="tpu_custom_call" | custom-call | tf_op jit(solution)/shard_map/lowered_block/pallas_call | solution.py:175
  26.3 2.2 %copy-done.1 = bf16[2048,1024]{1,0:T(8,128)(2,1)S(1)} copy-done((bf16[2048,1024]{1,0:T(8,128)(2,1)S(1)}, bf16[2048,1024]{1,0:T(8,128)(2,1)}, u32[]{:S(2)}) %copy-start.1) | copy-done | bytes 4194328
  28.4 2.0 %lowered_block.5 = bf16[128,2048]{1,0:T(8,128)(2,1)S(1)} custom-call(bf16[128,1024]{1,0:T(8,128)(2,1)S(1)} %collective-permute-done.2.cot_ref, bf16[2048,1024]{1,0:T(8,128)(2,1)S(1)} %copy-done.1), custom_call_target="tpu_custom_call" | custom-call | tf_op jit(solution)/shard_map/lowered_block/pallas_call | solution.py:175
  30.5 7.9 %collective-permute-start.11 = (bf16[128,2048]{1,0:T(8,128)(2,1)S(1)}, bf16[128,2048]{1,0:T(8,128)(2,1)S(1)}, u32[]{:S(2)}, u32[]{:S(2)}) collective-permute-start(bf16[128,2048]{1,0:T(8,128)(2,1)S(1)} %lowered_block.5), channel_id=1, source_target_pairs={{4,1},{5,0},{6,3},{7,2},{8,5},{9,4},{10,7},{11,6},{12,9},{13,8},{1... | collective-permute-start | bytes 1572872 | tf_op jit(solution)/shard_map/ppermute | solution.py:48
  38.4 2.8 %lowered_block.6 = bf16[128,2048]{1,0:T(8,128)(2,1)} custom-call(bf16[128,1024]{1,0:T(8,128)(2,1)S(1)} %broadcast_select_fusion.1.cot_ref, bf16[2048,1024]{1,0:T(8,128)(2,1)S(1)} %copy-done.1), custom_call_target="tpu_custom_call" | custom-call | tf_op jit(solution)/shard_map/lowered_block/pallas_call | solution.py:175
  41.3 4.1 %collective-permute-start.12 = (bf16[128,2048]{1,0:T(8,128)(2,1)}, bf16[128,2048]{1,0:T(8,128)(2,1)S(1)}, u32[]{:S(2)}, u32[]{:S(2)}) collective-permute-start(bf16[128,2048]{1,0:T(8,128)(2,1)} %lowered_block.6), channel_id=1, source_target_pairs={{4,2},{5,3},{6,0},{7,1},{8,6},{9,7},{10,4},{11,5},{12,10},{13,11},... | collective-permute-start | bytes 1572872 | tf_op jit(solution)/shard_map/ppermute | solution.py:48
  45.5 1.7 %broadcast_select_fusion.cot_ref = bf16[128,1024]{1,0:T(8,128)(2,1)} fusion(bf16[128,1024]{1,0:T(8,128)(2,1)S(1)} %collective-permute-done.8, bf16[128,1024]{1,0:T(8,128)(2,1)} %collective-permute-done.4, pred[]{:T(512)S(6)} %or.3), kind=kLoop, calls=%fused_computation.7 | loop fusion | flops 131072 | bytes 786433 | tf_op jit(solution)/shard_map/jit(_where)/select_n | solution.py:214
  47.2 3.8 %lowered_block.7 = bf16[128,2048]{1,0:T(8,128)(2,1)} custom-call(bf16[128,1024]{1,0:T(8,128)(2,1)} %broadcast_select_fusion.cot_ref, bf16[2048,1024]{1,0:T(8,128)(2,1)S(1)} %copy-done.1), custom_call_target="tpu_custom_call" | custom-call | tf_op jit(solution)/shard_map/lowered_block/pallas_call | solution.py:175
  51.0 3.0 %collective-permute-done.6 = bf16[128,2048]{1,0:T(8,128)(2,1)S(1)} collective-permute-done((bf16[128,2048]{1,0:T(8,128)(2,1)}, bf16[128,2048]{1,0:T(8,128)(2,1)S(1)}, u32[]{:S(2)}, u32[]{:S(2)}) %collective-permute-start.6) | collective-permute-done | bytes 524320 | tf_op jit(solution)/shard_map/ppermute | solution.py:27
  54.0 14.5 %collective-permute-start.13 = (bf16[128,2048]{1,0:T(8,128)(2,1)}, bf16[128,2048]{1,0:T(8,128)(2,1)}, u32[]{:S(2)}, u32[]{:S(2)}) collective-permute-start(bf16[128,2048]{1,0:T(8,128)(2,1)} %lowered_block.7), channel_id=1, source_target_pairs={{4,3},{5,2},{6,1},{7,0},{8,7},{9,6},{10,5},{11,4},{12,11},{13,10},... | collective-permute-start | bytes 1572872 | tf_op jit(solution)/shard_map/ppermute | solution.py:48
  68.5 1.9 %collective-permute-start.10 = (bf16[128,2048]{1,0:T(8,128)(2,1)S(1)}, bf16[128,2048]{1,0:T(8,128)(2,1)}, u32[]{:S(2)}, u32[]{:S(2)}) collective-permute-start(bf16[128,2048]{1,0:T(8,128)(2,1)S(1)} %lowered_block.4), channel_id=1, source_target_pairs={{4,0},{5,1},{6,2},{7,3},{8,4},{9,5},{10,6},{11,7},{12,8},{13,9},{1... | collective-permute-start | bytes 1572872 | tf_op jit(solution)/shard_map/ppermute | solution.py:48
  70.5 10.3 %collective-permute-done.5 = bf16[128,2048]{1,0:T(8,128)(2,1)} collective-permute-done((bf16[128,2048]{1,0:T(8,128)(2,1)}, bf16[128,2048]{1,0:T(8,128)(2,1)}, u32[]{:S(2)}, u32[]{:S(2)}) %collective-permute-start.5) | collective-permute-done | bytes 524320 | tf_op jit(solution)/shard_map/ppermute | solution.py:27
  80.7 30.3 %conditional.1 = (f32[2048,1024]{1,0:T(8,128)S(1)}, f32[8,1024]{1,0:T(8,128)S(1)}, f32[2048]{0:T(1024)}) conditional(s32[]{:T(128)} %convert_element_type.12, () %tuple.25, (bf16[128,2048]{1,0:T(8,128)(2,1)}, bf16[128,2048]{1,0:T(8,128)(2,1)}, bf16[128,2048]{1,0:T(8,128)(2,1)S(1)}, bf16[128,2048]{1,0:T(8,128)(2,1)}, bf16[128,1024]{1,0:T(8,128)(2,1)S(1)}, ...), branch_computations={%region_0.1_spmd, %region_1.2_spmd} | conditional | flops 16384 | bytes 8429604 | solution.py:242
  81.9 5.8 %gradient_and_sums.1 = (f32[2048,1024]{1,0:T(8,128)S(1)}, f32[1,2048]{1,0:T(1,128)}, f32[8,1024]{1,0:T(8,128)S(1)}) custom-call(bf16[128,2048]{1,0:T(8,128)(2,1)} %get-tuple-element.19.refs_0_, bf16[128,2048]{1,0:T(8,128)(2,1)} %get-tuple-element.20.refs_1_, bf16[128,2048]{1,0:T(8,128)(2,1)} %copy-done.5, bf16[128,2048]{1,0:T(8,128)(2,1)} %get-tuple-element.22.refs_3_, ...), custom_call_target="tpu_custom_call" | custom-call | tf_op jit(solution)/shard_map/cond/branch_1_fun/gradient_and_sums/pallas_call | solution.py:88
  87.7 6.9 %collective-permute-start = (f32[8,1024]{1,0:T(8,128)S(1)}, f32[8,1024]{1,0:T(8,128)S(1)}, u32[]{:S(2)}, u32[]{:S(2)}) collective-permute-start(f32[8,1024]{1,0:T(8,128)S(1)} %get-tuple-element.29), channel_id=1, source_target_pairs={{0,1},{1,0},{2,3},{3,2},{4,5},{5,4},{6,7},{7,6},{8,9},{9,8},{10,11... | collective-permute-start | bytes 98312 | tf_op jit(solution)/shard_map/cond/branch_1_fun/ppermute | solution.py:36
  94.5 5.4 %collective-permute-done = f32[8,1024]{1,0:T(8,128)S(1)} collective-permute-done((f32[8,1024]{1,0:T(8,128)S(1)}, f32[8,1024]{1,0:T(8,128)S(1)}, u32[]{:S(2)}, u32[]{:S(2)}) %collective-permute-start) | collective-permute-done | bytes 32800 | tf_op jit(solution)/shard_map/cond/branch_1_fun/ppermute | solution.py:36
  99.9 11.0 %collective-permute-done.1 = f32[8,1024]{1,0:T(8,128)S(1)} collective-permute-done((f32[8,1024]{1,0:T(8,128)S(1)}, f32[8,1024]{1,0:T(8,128)S(1)}, u32[]{:S(2)}, u32[]{:S(2)}) %collective-permute-start.1) | collective-permute-done | bytes 32800 | tf_op jit(solution)/shard_map/cond/branch_1_fun/ppermute | solution.py:36
  111.0 4.4 %finish.1 = (bf16[2048,1024]{1,0:T(8,128)(2,1)}, f32[1,1024]{1,0:T(1,128)}, bf16[128,8192]{1,0:T(8,128)(2,1)}) custom-call(s32[1]{0:T(128)} %bitcast.1.me_ref, f32[8,1024]{1,0:T(8,128)S(1)} %get-tuple-element.53.sums_ref, f32[1,1024]{1,0:T(1,128)S(1)} %bitcast.5, f32[2048,1024]{1,0:T(8,128)S(1)} %get-tuple-element.54.scaled_ref, ...), custom_call_target="tpu_custom_call" | custom-call | tf_op jit(solution)/shard_map/finish/pallas_call | solution.py:138
  (32 shorter events, 6.8 us)
Async XLA Ops:
  1.8 7.2 %collective-permute-start.2 = (bf16[128,1024]{1,0:T(8,128)(2,1)S(1)}, bf16[128,1024]{1,0:T(8,128)(2,1)S(1)}, u32[]{:S(2)}, u32[]{:S(2)}) collective-permute-start(bf16[128,1024]{1,0:T(8,128)(2,1)S(1)} %fusion.4.cot_ref), channel_id=1, source_target_pairs={{0,1},{1,0},{2,3},{3,2},{4,5},{5,4},{6,7},{7,6},{8,9},{9,8},{10,11... | collective-permute-start | bytes 786440 | tf_op jit(solution)/shard_map/ppermute | solution.py:27
  3.2 7.2 %collective-permute-start.8 = (bf16[128,1024]{1,0:T(8,128)(2,1)S(1)}, bf16[128,1024]{1,0:T(8,128)(2,1)S(1)}, u32[]{:S(2)}, u32[]{:S(2)}) collective-permute-start(bf16[128,1024]{1,0:T(8,128)(2,1)S(1)} %fusion.4.cot_ref), channel_id=1, source_target_pairs={{1,2},{2,1},{5,6},{6,5},{9,10},{10,9},{13,14},{14,13},{17,18},{18,... | collective-permute-start | bytes 786440 | tf_op jit(solution)/shard_map/ppermute | solution.py:209
  9.1 17.2 %copy-start.4 = (bf16[128,1024]{1,0:T(8,128)(2,1)}, bf16[128,1024]{1,0:T(8,128)(2,1)S(1)}, u32[]{:S(2)}) copy-start(bf16[128,1024]{1,0:T(8,128)(2,1)S(1)} %collective-permute-done.2.cot_ref) | copy-start | bytes 786436
  9.1 5.5 %collective-permute-start.3 = (bf16[128,1024]{1,0:T(8,128)(2,1)S(1)}, bf16[128,1024]{1,0:T(8,128)(2,1)}, u32[]{:S(2)}, u32[]{:S(2)}) collective-permute-start(bf16[128,1024]{1,0:T(8,128)(2,1)S(1)} %collective-permute-done.2.cot_ref), channel_id=1, source_target_pairs={{1,2},{2,1},{5,6},{6,5},{9,10},{10,9},{13,14},{14,13},{17,18},{18,... | collective-permute-start | bytes 786440 | tf_op jit(solution)/shard_map/ppermute | solution.py:210
  10.4 27.9 %collective-permute-start.9 = (bf16[128,1024]{1,0:T(8,128)(2,1)S(1)}, bf16[128,1024]{1,0:T(8,128)(2,1)S(1)}, u32[]{:S(2)}, u32[]{:S(2)}) collective-permute-start(bf16[128,1024]{1,0:T(8,128)(2,1)S(1)} %collective-permute-done.8), channel_id=1, source_target_pairs={{1,0},{2,3},{5,4},{6,7},{9,8},{10,11},{13,12},{14,15},{17,16},{18,... | collective-permute-start | bytes 786440 | tf_op jit(solution)/shard_map/ppermute | solution.py:211
  14.6 39.4 %collective-permute-start.6 = (bf16[128,2048]{1,0:T(8,128)(2,1)}, bf16[128,2048]{1,0:T(8,128)(2,1)S(1)}, u32[]{:S(2)}, u32[]{:S(2)}) collective-permute-start(bf16[128,2048]{1,0:T(8,128)(2,1)} %get-tuple-element.50), channel_id=1, source_target_pairs={{0,2},{1,3},{2,0},{3,1},{4,6},{5,7},{6,4},{7,5},{8,10},{9,11},{10,... | collective-permute-start | bytes 1572872 | tf_op jit(solution)/shard_map/ppermute | solution.py:27
  19.6 34.4 %collective-permute-start.7 = (bf16[128,2048]{1,0:T(8,128)(2,1)}, bf16[128,2048]{1,0:T(8,128)(2,1)}, u32[]{:S(2)}, u32[]{:S(2)}) collective-permute-start(bf16[128,2048]{1,0:T(8,128)(2,1)} %get-tuple-element.51), channel_id=1, source_target_pairs={{0,3},{1,2},{2,1},{3,0},{4,7},{5,6},{6,5},{7,4},{8,11},{9,10},{10,... | collective-permute-start | bytes 1572872 | tf_op jit(solution)/shard_map/ppermute | solution.py:27
  20.7 24.7 %collective-permute-start.4 = (bf16[128,1024]{1,0:T(8,128)(2,1)}, bf16[128,1024]{1,0:T(8,128)(2,1)}, u32[]{:S(2)}, u32[]{:S(2)}) collective-permute-start(bf16[128,1024]{1,0:T(8,128)(2,1)} %collective-permute-done.3), channel_id=1, source_target_pairs={{1,0},{2,3},{5,4},{6,7},{9,8},{10,11},{13,12},{14,15},{17,16},{18,... | collective-permute-start | bytes 786440 | tf_op jit(solution)/shard_map/ppermute | solution.py:212
  22.0 2.2 %copy-start = (bf16[2048,1024]{1,0:T(8,128)(2,1)S(1)}, bf16[2048,1024]{1,0:T(8,128)(2,1)}, u32[]{:S(2)}) copy-start(bf16[2048,1024]{1,0:T(8,128)(2,1)} %weight_ref.7) | copy-start | bytes 12582916
  26.3 2.2 %copy-start.1 = (bf16[2048,1024]{1,0:T(8,128)(2,1)S(1)}, bf16[2048,1024]{1,0:T(8,128)(2,1)}, u32[]{:S(2)}) copy-start(bf16[2048,1024]{1,0:T(8,128)(2,1)} %weight_ref.7) | copy-start | bytes 12582916
  30.5 80.5 %collective-permute-start.11 = (bf16[128,2048]{1,0:T(8,128)(2,1)S(1)}, bf16[128,2048]{1,0:T(8,128)(2,1)S(1)}, u32[]{:S(2)}, u32[]{:S(2)}) collective-permute-start(bf16[128,2048]{1,0:T(8,128)(2,1)S(1)} %lowered_block.5), channel_id=1, source_target_pairs={{4,1},{5,0},{6,3},{7,2},{8,5},{9,4},{10,7},{11,6},{12,9},{13,8},{1... | collective-permute-start | bytes 1572872 | tf_op jit(solution)/shard_map/ppermute | solution.py:48
  38.4 42.3 %copy-start.3 = (bf16[128,1024]{1,0:T(8,128)(2,1)}, bf16[128,1024]{1,0:T(8,128)(2,1)S(1)}, u32[]{:S(2)}) copy-start(bf16[128,1024]{1,0:T(8,128)(2,1)S(1)} %broadcast_select_fusion.1.cot_ref) | copy-start | bytes 786436
  38.4 42.3 %copy-start.6 = (f32[2048]{0:T(1024)S(1)}, f32[2048]{0:T(1024)}, u32[]{:S(2)}) copy-start(f32[2048]{0:T(1024)} %param.12) | copy-start | bytes 24580
  41.3 69.7 %collective-permute-start.12 = (bf16[128,2048]{1,0:T(8,128)(2,1)}, bf16[128,2048]{1,0:T(8,128)(2,1)S(1)}, u32[]{:S(2)}, u32[]{:S(2)}) collective-permute-start(bf16[128,2048]{1,0:T(8,128)(2,1)} %lowered_block.6), channel_id=1, source_target_pairs={{4,2},{5,3},{6,0},{7,1},{8,6},{9,7},{10,4},{11,5},{12,10},{13,11},... | collective-permute-start | bytes 1572872 | tf_op jit(solution)/shard_map/ppermute | solution.py:48
  45.4 35.3 %collective-permute-start.5 = (bf16[128,2048]{1,0:T(8,128)(2,1)}, bf16[128,2048]{1,0:T(8,128)(2,1)}, u32[]{:S(2)}, u32[]{:S(2)}) collective-permute-start(bf16[128,2048]{1,0:T(8,128)(2,1)} %get-tuple-element.49), channel_id=1, source_target_pairs={{0,1},{1,0},{2,3},{3,2},{4,5},{5,4},{6,7},{7,6},{8,9},{9,8},{10,11... | collective-permute-start | bytes 1572872 | tf_op jit(solution)/shard_map/ppermute | solution.py:27
  54.0 57.0 %collective-permute-start.13 = (bf16[128,2048]{1,0:T(8,128)(2,1)}, bf16[128,2048]{1,0:T(8,128)(2,1)}, u32[]{:S(2)}, u32[]{:S(2)}) collective-permute-start(bf16[128,2048]{1,0:T(8,128)(2,1)} %lowered_block.7), channel_id=1, source_target_pairs={{4,3},{5,2},{6,1},{7,0},{8,7},{9,6},{10,5},{11,4},{12,11},{13,10},... | collective-permute-start | bytes 1572872 | tf_op jit(solution)/shard_map/ppermute | solution.py:48
  68.5 42.5 %collective-permute-start.10 = (bf16[128,2048]{1,0:T(8,128)(2,1)S(1)}, bf16[128,2048]{1,0:T(8,128)(2,1)}, u32[]{:S(2)}, u32[]{:S(2)}) collective-permute-start(bf16[128,2048]{1,0:T(8,128)(2,1)S(1)} %lowered_block.4), channel_id=1, source_target_pairs={{4,0},{5,1},{6,2},{7,3},{8,4},{9,5},{10,6},{11,7},{12,8},{13,9},{1... | collective-permute-start | bytes 1572872 | tf_op jit(solution)/shard_map/ppermute | solution.py:48
  80.7 30.3 %copy-start.2 = (f32[1024]{0:T(1024)S(1)}, f32[1024]{0:T(1024)}, u32[]{:S(2)}) copy-start(f32[1024]{0:T(1024)} %param.13) | copy-start | bytes 12292
  80.7 0.8 copy-start.5
  87.7 12.3 %collective-permute-start = (f32[8,1024]{1,0:T(8,128)S(1)}, f32[8,1024]{1,0:T(8,128)S(1)}, u32[]{:S(2)}, u32[]{:S(2)}) collective-permute-start(f32[8,1024]{1,0:T(8,128)S(1)} %get-tuple-element.29), channel_id=1, source_target_pairs={{0,1},{1,0},{2,3},{3,2},{4,5},{5,4},{6,7},{7,6},{8,9},{9,8},{10,11... | collective-permute-start | bytes 98312 | tf_op jit(solution)/shard_map/cond/branch_1_fun/ppermute | solution.py:36
  99.9 11.0 %collective-permute-start.1 = (f32[8,1024]{1,0:T(8,128)S(1)}, f32[8,1024]{1,0:T(8,128)S(1)}, u32[]{:S(2)}, u32[]{:S(2)}) collective-permute-start(f32[8,1024]{1,0:T(8,128)S(1)} %add.15), channel_id=1, source_target_pairs={{0,2},{1,3},{2,0},{3,1},{4,6},{5,7},{6,4},{7,5},{8,10},{9,11},{10,... | collective-permute-start | bytes 98312 | tf_op jit(solution)/shard_map/cond/branch_1_fun/ppermute | solution.py:36

commit v5 on v3

--- a/solution.py
+++ b/solution.py
@@ -211,7 +211,7 @@
         third = lax.ppermute(across, DP, outward)
         cots[2] = jnp.where(is_inner, across, second)
         cots[3] = jnp.where(is_inner, middle, third)
-        first, nearest = (across,), (third,)
+        first, nearest = (across,), (third, second)
     else:
         for k in range(1, count):
             cots[k] = trade(cotangent, k)

time: 117 us -> 117 us (level)
  no operation moved by 1% of the time
where the time goes in v5:
time: 117 us; the launch traced here: 115 us
  starting transfers between devices  44.7 us (38%)
  waiting for transfers between devices  38.8 us (33%)
  Pallas kernels  20.9 us (18%)
  local copies, waits for them, and re-layouts  6.25 us (5%)
  other arithmetic  3.9 us (3%)
    ppermute x4, waiting for transfers between devices, trade(): lax.ppermute(value, DP, [(i, partner(steps, i, count)) for i in range(cou...  30.2 us
    ppermute x4, starting transfers between devices, hand_over(): return lax.ppermute(value, (SECTION, DP), pairs)  18.5 us
    ppermute x2, starting transfers between devices, everyone(): lax.ppermute(value, DP, [(i, i ^ reach_of) for i in range(count)])  14.1 us
    pallas_call x4, Pallas kernels, lowered(): pl.pallas_call(lowered_kernel, grid=(rows // block,), in_specs=[pl.BlockS...  10.7 us
    ppermute x2, waiting for transfers between devices, everyone(): lax.ppermute(value, DP, [(i, i ^ reach_of) for i in range(count)])  8.59 us
    ppermute x4, starting transfers between devices, trade(): lax.ppermute(value, DP, [(i, partner(steps, i, count)) for i in range(cou...  7.53 us
    pallas_call x1, Pallas kernels, gradient_call(): pl.pallas_call(functools.partial(gradient_kernel, parts, min(256, block))...  5.77 us
    pallas_call x1, Pallas kernels, finish(): pl.pallas_call(functools.partial(finish_kernel, float(width), count), gri...  4.43 us
  transfers between devices with their start and end apart: 14, of which 5 were waited for; matrix products, arithmetic and copies ran while one was open for 5% of the time, Pallas kernels for 14%

profile of v5, /device:TPU:3, one launch (start us, length us, event | category | flops | bytes accessed | tf_op | source)
XLA Modules:
  0.0 115.5 jit_solution(8113396476983898513)
XLA Ops:
  1.8 1.4 %collective-permute-start.2 = (bf16[128,1024]{1,0:T(8,128)(2,1)S(1)}, bf16[128,1024]{1,0:T(8,128)(2,1)S(1)}, u32[]{:S(2)}, u32[]{:S(2)}) collective-permute-start(bf16[128,1024]{1,0:T(8,128)(2,1)S(1)} %fusion.4.cot_ref), channel_id=1, source_target_pairs={{0,1},{1,0},{2,3},{3,2},{4,5},{5,4},{6,7},{7,6},{8,9},{9,8},{10,11... | collective-permute-start | bytes 786440 | tf_op jit(solution)/shard_map/ppermute | solution.py:27
  3.9 5.2 %collective-permute-done.2.cot_ref = bf16[128,1024]{1,0:T(8,128)(2,1)S(1)} collective-permute-done((bf16[128,1024]{1,0:T(8,128)(2,1)S(1)}, bf16[128,1024]{1,0:T(8,128)(2,1)S(1)}, u32[]{:S(2)}, u32[]{:S(2)}) %collective-permute-start.2) | collective-permute-done | bytes 262176 | tf_op jit(solution)/shard_map/ppermute | solution.py:27
  9.1 1.4 %collective-permute-start.3 = (bf16[128,1024]{1,0:T(8,128)(2,1)S(1)}, bf16[128,1024]{1,0:T(8,128)(2,1)}, u32[]{:S(2)}, u32[]{:S(2)}) collective-permute-start(bf16[128,1024]{1,0:T(8,128)(2,1)S(1)} %collective-permute-done.2.cot_ref), channel_id=1, source_target_pairs={{1,2},{2,1},{5,6},{6,5},{9,10},{10,9},{13,14},{14,13},{17,18},{18,... | collective-permute-start | bytes 786440 | tf_op jit(solution)/shard_map/ppermute | solution.py:209
  11.7 2.9 %constant_dynamic-slice_fusion = (bf16[128,2048]{1,0:T(8,128)(2,1)}, bf16[128,2048]{1,0:T(8,128)(2,1)}, bf16[128,2048]{1,0:T(8,128)(2,1)}, bf16[128,2048]{1,0:T(8,128)(2,1)}) fusion(bf16[128,8192]{1,0:T(8,128)(2,1)} %param.8, s32[]{:T(128)S(6)} %select_n.27, s32[]{:T(128)S(6)} %select_n.25, s32[]{:T(128)S(6)} %select_n.24, s32[]{:T(128)S(6)} %select_n.26), kind=kLoop, calls=%fused_computation.9 | loop fusion | bytes 4194320 | tf_op jit(solution)/shard_map/dynamic_slice | solution.py:197
  14.6 5.0 %collective-permute-start.8 = (bf16[128,2048]{1,0:T(8,128)(2,1)}, bf16[128,2048]{1,0:T(8,128)(2,1)S(1)}, u32[]{:S(2)}, u32[]{:S(2)}) collective-permute-start(bf16[128,2048]{1,0:T(8,128)(2,1)} %get-tuple-element.48), channel_id=1, source_target_pairs={{0,2},{1,3},{2,0},{3,1},{4,6},{5,7},{6,4},{7,5},{8,10},{9,11},{10,... | collective-permute-start | bytes 1572872 | tf_op jit(solution)/shard_map/ppermute | solution.py:27
  22.0 2.0 %lowered_block.4 = bf16[128,2048]{1,0:T(8,128)(2,1)S(1)} custom-call(bf16[128,1024]{1,0:T(8,128)(2,1)S(1)} %fusion.4.cot_ref, bf16[2048,1024]{1,0:T(8,128)(2,1)S(1)} %copy-done), custom_call_target="tpu_custom_call" | custom-call | tf_op jit(solution)/shard_map/lowered_block/pallas_call | solution.py:175
  24.0 4.9 %collective-permute-start.10 = (bf16[128,2048]{1,0:T(8,128)(2,1)S(1)}, bf16[128,2048]{1,0:T(8,128)(2,1)S(1)}, u32[]{:S(2)}, u32[]{:S(2)}) collective-permute-start(bf16[128,2048]{1,0:T(8,128)(2,1)S(1)} %lowered_block.4), channel_id=1, source_target_pairs={{4,0},{5,1},{6,2},{7,3},{8,4},{9,5},{10,6},{11,7},{12,8},{13,9},{1... | collective-permute-start | bytes 1572872 | tf_op jit(solution)/shard_map/ppermute | solution.py:48
  29.0 2.2 %copy-done.1 = bf16[2048,1024]{1,0:T(8,128)(2,1)S(1)} copy-done((bf16[2048,1024]{1,0:T(8,128)(2,1)S(1)}, bf16[2048,1024]{1,0:T(8,128)(2,1)}, u32[]{:S(2)}) %copy-start.1) | copy-done | bytes 4194328
  31.2 2.0 %lowered_block.5 = bf16[128,2048]{1,0:T(8,128)(2,1)S(1)} custom-call(bf16[128,1024]{1,0:T(8,128)(2,1)S(1)} %collective-permute-done.2.cot_ref, bf16[2048,1024]{1,0:T(8,128)(2,1)S(1)} %copy-done.1), custom_call_target="tpu_custom_call" | custom-call | tf_op jit(solution)/shard_map/lowered_block/pallas_call | solution.py:175
  33.2 4.9 %collective-permute-start.11 = (bf16[128,2048]{1,0:T(8,128)(2,1)S(1)}, bf16[128,2048]{1,0:T(8,128)(2,1)S(1)}, u32[]{:S(2)}, u32[]{:S(2)}) collective-permute-start(bf16[128,2048]{1,0:T(8,128)(2,1)S(1)} %lowered_block.5), channel_id=1, source_target_pairs={{4,1},{5,0},{6,3},{7,2},{8,5},{9,4},{10,7},{11,6},{12,9},{13,8},{1... | collective-permute-start | bytes 1572872 | tf_op jit(solution)/shard_map/ppermute | solution.py:48
  39.1 2.9 %lowered_block.6 = bf16[128,2048]{1,0:T(8,128)(2,1)} custom-call(bf16[128,1024]{1,0:T(8,128)(2,1)S(1)} %broadcast_select_fusion.1.cot_ref, bf16[2048,1024]{1,0:T(8,128)(2,1)S(1)} %copy-done.1), custom_call_target="tpu_custom_call" | custom-call | tf_op jit(solution)/shard_map/lowered_block/pallas_call | solution.py:175
  42.1 1.7 %broadcast_select_fusion.cot_ref = bf16[128,1024]{1,0:T(8,128)(2,1)} fusion(bf16[128,1024]{1,0:T(8,128)(2,1)S(1)} %collective-permute-done.5, bf16[128,1024]{1,0:T(8,128)(2,1)} %collective-permute-done.4, pred[]{:T(512)S(6)} %or.3), kind=kLoop, calls=%fused_computation.7 | loop fusion | flops 131072 | bytes 786433 | tf_op jit(solution)/shard_map/jit(_where)/select_n | solution.py:213
  43.8 3.8 %lowered_block.7 = bf16[128,2048]{1,0:T(8,128)(2,1)} custom-call(bf16[128,1024]{1,0:T(8,128)(2,1)} %broadcast_select_fusion.cot_ref, bf16[2048,1024]{1,0:T(8,128)(2,1)S(1)} %copy-done.1), custom_call_target="tpu_custom_call" | custom-call | tf_op jit(solution)/shard_map/lowered_block/pallas_call | solution.py:175
  47.6 6.1 %collective-permute-done.8 = bf16[128,2048]{1,0:T(8,128)(2,1)S(1)} collective-permute-done((bf16[128,2048]{1,0:T(8,128)(2,1)}, bf16[128,2048]{1,0:T(8,128)(2,1)S(1)}, u32[]{:S(2)}, u32[]{:S(2)}) %collective-permute-start.8) | collective-permute-done | bytes 524320 | tf_op jit(solution)/shard_map/ppermute | solution.py:27
  53.7 3.9 %collective-permute-start.12 = (bf16[128,2048]{1,0:T(8,128)(2,1)}, bf16[128,2048]{1,0:T(8,128)(2,1)}, u32[]{:S(2)}, u32[]{:S(2)}) collective-permute-start(bf16[128,2048]{1,0:T(8,128)(2,1)} %lowered_block.6), channel_id=1, source_target_pairs={{4,2},{5,3},{6,0},{7,1},{8,6},{9,7},{10,4},{11,5},{12,10},{13,11},... | collective-permute-start | bytes 1572872 | tf_op jit(solution)/shard_map/ppermute | solution.py:48
  57.6 4.7 %collective-permute-start.13 = (bf16[128,2048]{1,0:T(8,128)(2,1)}, bf16[128,2048]{1,0:T(8,128)(2,1)}, u32[]{:S(2)}, u32[]{:S(2)}) collective-permute-start(bf16[128,2048]{1,0:T(8,128)(2,1)} %lowered_block.7), channel_id=1, source_target_pairs={{4,3},{5,2},{6,1},{7,0},{8,7},{9,6},{10,5},{11,4},{12,11},{13,10},... | collective-permute-start | bytes 1572872 | tf_op jit(solution)/shard_map/ppermute | solution.py:48
  62.4 18.9 %collective-permute-done.7 = bf16[128,2048]{1,0:T(8,128)(2,1)} collective-permute-done((bf16[128,2048]{1,0:T(8,128)(2,1)}, bf16[128,2048]{1,0:T(8,128)(2,1)}, u32[]{:S(2)}, u32[]{:S(2)}) %collective-permute-start.7) | collective-permute-done | bytes 524320 | tf_op jit(solution)/shard_map/ppermute | solution.py:27
  81.3 29.6 %conditional.1 = (f32[2048,1024]{1,0:T(8,128)S(1)}, f32[8,1024]{1,0:T(8,128)S(1)}, f32[2048]{0:T(1024)}) conditional(s32[]{:T(128)} %convert_element_type.12, () %tuple.23, (f32[2048]{0:T(1024)S(1)}, bf16[128,2048]{1,0:T(8,128)(2,1)}, bf16[128,2048]{1,0:T(8,128)(2,1)}, bf16[128,2048]{1,0:T(8,128)(2,1)S(1)}, bf16[128,2048]{1,0:T(8,128)(2,1)}, ...), branch_computations={%region_0.1_spmd, %region_1.2_spmd} | conditional | flops 16384 | bytes 8429604 | solution.py:241
  82.5 5.8 %gradient_and_sums.1 = (f32[2048,1024]{1,0:T(8,128)S(1)}, f32[1,2048]{1,0:T(1,128)}, f32[8,1024]{1,0:T(8,128)S(1)}) custom-call(bf16[128,2048]{1,0:T(8,128)(2,1)} %get-tuple-element.19.refs_0_, bf16[128,2048]{1,0:T(8,128)(2,1)} %get-tuple-element.20.refs_1_, bf16[128,2048]{1,0:T(8,128)(2,1)} %copy-done.5, bf16[128,2048]{1,0:T(8,128)(2,1)} %get-tuple-element.22.refs_3_, ...), custom_call_target="tpu_custom_call" | custom-call | tf_op jit(solution)/shard_map/cond/branch_1_fun/gradient_and_sums/pallas_call | solution.py:88
  88.3 12.4 %collective-permute-start = (f32[8,1024]{1,0:T(8,128)S(1)}, f32[8,1024]{1,0:T(8,128)S(1)}, u32[]{:S(2)}, u32[]{:S(2)}) collective-permute-start(f32[8,1024]{1,0:T(8,128)S(1)} %get-tuple-element.29), channel_id=1, source_target_pairs={{0,1},{1,0},{2,3},{3,2},{4,5},{5,4},{6,7},{7,6},{8,9},{9,8},{10,11... | collective-permute-start | bytes 98312 | tf_op jit(solution)/shard_map/cond/branch_1_fun/ppermute | solution.py:36
  100.6 1.3 %collective-permute-done = f32[8,1024]{1,0:T(8,128)S(1)} collective-permute-done((f32[8,1024]{1,0:T(8,128)S(1)}, f32[8,1024]{1,0:T(8,128)S(1)}, u32[]{:S(2)}, u32[]{:S(2)}) %collective-permute-start) | collective-permute-done | bytes 32800 | tf_op jit(solution)/shard_map/cond/branch_1_fun/ppermute | solution.py:36
  101.9 1.8 %collective-permute-start.1 = (f32[8,1024]{1,0:T(8,128)S(1)}, f32[8,1024]{1,0:T(8,128)S(1)}, u32[]{:S(2)}, u32[]{:S(2)}) collective-permute-start(f32[8,1024]{1,0:T(8,128)S(1)} %add.15), channel_id=1, source_target_pairs={{0,2},{1,3},{2,0},{3,1},{4,6},{5,7},{6,4},{7,5},{8,10},{9,11},{10,... | collective-permute-start | bytes 98312 | tf_op jit(solution)/shard_map/cond/branch_1_fun/ppermute | solution.py:36
  103.7 7.3 %collective-permute-done.1 = f32[8,1024]{1,0:T(8,128)S(1)} collective-permute-done((f32[8,1024]{1,0:T(8,128)S(1)}, f32[8,1024]{1,0:T(8,128)S(1)}, u32[]{:S(2)}, u32[]{:S(2)}) %collective-permute-start.1) | collective-permute-done | bytes 32800 | tf_op jit(solution)/shard_map/cond/branch_1_fun/ppermute | solution.py:36
  111.0 4.4 %finish.1 = (bf16[2048,1024]{1,0:T(8,128)(2,1)}, f32[1,1024]{1,0:T(1,128)}, bf16[128,8192]{1,0:T(8,128)(2,1)}) custom-call(s32[1]{0:T(128)} %bitcast.2.me_ref, f32[8,1024]{1,0:T(8,128)S(1)} %get-tuple-element.50.sums_ref, f32[1,1024]{1,0:T(1,128)S(1)} %bitcast.5, f32[2048,1024]{1,0:T(8,128)S(1)} %get-tuple-element.51.scaled_ref, ...), custom_call_target="tpu_custom_call" | custom-call | tf_op jit(solution)/shard_map/finish/pallas_call | solution.py:138
  (32 shorter events, 7.8 us)
Async XLA Ops:
  1.8 7.2 %collective-permute-start.2 = (bf16[128,1024]{1,0:T(8,128)(2,1)S(1)}, bf16[128,1024]{1,0:T(8,128)(2,1)S(1)}, u32[]{:S(2)}, u32[]{:S(2)}) collective-permute-start(bf16[128,1024]{1,0:T(8,128)(2,1)S(1)} %fusion.4.cot_ref), channel_id=1, source_target_pairs={{0,1},{1,0},{2,3},{3,2},{4,5},{5,4},{6,7},{7,6},{8,9},{9,8},{10,11... | collective-permute-start | bytes 786440 | tf_op jit(solution)/shard_map/ppermute | solution.py:27
  3.2 7.2 %collective-permute-start.5 = (bf16[128,1024]{1,0:T(8,128)(2,1)S(1)}, bf16[128,1024]{1,0:T(8,128)(2,1)S(1)}, u32[]{:S(2)}, u32[]{:S(2)}) collective-permute-start(bf16[128,1024]{1,0:T(8,128)(2,1)S(1)} %fusion.4.cot_ref), channel_id=1, source_target_pairs={{1,2},{2,1},{5,6},{6,5},{9,10},{10,9},{13,14},{14,13},{17,18},{18,... | collective-permute-start | bytes 786440 | tf_op jit(solution)/shard_map/ppermute | solution.py:208
  3.9 18.1 %copy-start = (bf16[2048,1024]{1,0:T(8,128)(2,1)S(1)}, bf16[2048,1024]{1,0:T(8,128)(2,1)}, u32[]{:S(2)}) copy-start(bf16[2048,1024]{1,0:T(8,128)(2,1)} %weight_ref.7) | copy-start | bytes 12582916
  9.1 19.9 %copy-start.4 = (bf16[128,1024]{1,0:T(8,128)(2,1)}, bf16[128,1024]{1,0:T(8,128)(2,1)S(1)}, u32[]{:S(2)}) copy-start(bf16[128,1024]{1,0:T(8,128)(2,1)S(1)} %collective-permute-done.2.cot_ref) | copy-start | bytes 786436
  9.1 5.5 %collective-permute-start.3 = (bf16[128,1024]{1,0:T(8,128)(2,1)S(1)}, bf16[128,1024]{1,0:T(8,128)(2,1)}, u32[]{:S(2)}, u32[]{:S(2)}) collective-permute-start(bf16[128,1024]{1,0:T(8,128)(2,1)S(1)} %collective-permute-done.2.cot_ref), channel_id=1, source_target_pairs={{1,2},{2,1},{5,6},{6,5},{9,10},{10,9},{13,14},{14,13},{17,18},{18,... | collective-permute-start | bytes 786440 | tf_op jit(solution)/shard_map/ppermute | solution.py:209
  10.4 22.8 %collective-permute-start.6 = (bf16[128,1024]{1,0:T(8,128)(2,1)S(1)}, bf16[128,1024]{1,0:T(8,128)(2,1)}, u32[]{:S(2)}, u32[]{:S(2)}) collective-permute-start(bf16[128,1024]{1,0:T(8,128)(2,1)S(1)} %collective-permute-done.5), channel_id=1, source_target_pairs={{1,0},{2,3},{5,4},{6,7},{9,8},{10,11},{13,12},{14,15},{17,16},{18,... | collective-permute-start | bytes 786440 | tf_op jit(solution)/shard_map/ppermute | solution.py:210
  14.6 39.1 %collective-permute-start.8 = (bf16[128,2048]{1,0:T(8,128)(2,1)}, bf16[128,2048]{1,0:T(8,128)(2,1)S(1)}, u32[]{:S(2)}, u32[]{:S(2)}) collective-permute-start(bf16[128,2048]{1,0:T(8,128)(2,1)} %get-tuple-element.48), channel_id=1, source_target_pairs={{0,2},{1,3},{2,0},{3,1},{4,6},{5,7},{6,4},{7,5},{8,10},{9,11},{10,... | collective-permute-start | bytes 1572872 | tf_op jit(solution)/shard_map/ppermute | solution.py:27
  19.6 38.0 %collective-permute-start.9 = (bf16[128,2048]{1,0:T(8,128)(2,1)}, bf16[128,2048]{1,0:T(8,128)(2,1)}, u32[]{:S(2)}, u32[]{:S(2)}) collective-permute-start(bf16[128,2048]{1,0:T(8,128)(2,1)} %get-tuple-element.49), channel_id=1, source_target_pairs={{0,3},{1,2},{2,1},{3,0},{4,7},{5,6},{6,5},{7,4},{8,11},{9,10},{10,... | collective-permute-start | bytes 1572872 | tf_op jit(solution)/shard_map/ppermute | solution.py:27
  20.7 21.3 %collective-permute-start.4 = (bf16[128,1024]{1,0:T(8,128)(2,1)}, bf16[128,1024]{1,0:T(8,128)(2,1)}, u32[]{:S(2)}, u32[]{:S(2)}) collective-permute-start(bf16[128,1024]{1,0:T(8,128)(2,1)} %collective-permute-done.3), channel_id=1, source_target_pairs={{1,0},{2,3},{5,4},{6,7},{9,8},{10,11},{13,12},{14,15},{17,16},{18,... | collective-permute-start | bytes 786440 | tf_op jit(solution)/shard_map/ppermute | solution.py:211
  24.0 86.9 %collective-permute-start.10 = (bf16[128,2048]{1,0:T(8,128)(2,1)S(1)}, bf16[128,2048]{1,0:T(8,128)(2,1)S(1)}, u32[]{:S(2)}, u32[]{:S(2)}) collective-permute-start(bf16[128,2048]{1,0:T(8,128)(2,1)S(1)} %lowered_block.4), channel_id=1, source_target_pairs={{4,0},{5,1},{6,2},{7,3},{8,4},{9,5},{10,6},{11,7},{12,8},{13,9},{1... | collective-permute-start | bytes 1572872 | tf_op jit(solution)/shard_map/ppermute | solution.py:48
  29.0 2.2 %copy-start.1 = (bf16[2048,1024]{1,0:T(8,128)(2,1)S(1)}, bf16[2048,1024]{1,0:T(8,128)(2,1)}, u32[]{:S(2)}) copy-start(bf16[2048,1024]{1,0:T(8,128)(2,1)} %weight_ref.7) | copy-start | bytes 12582916
  33.2 77.8 %collective-permute-start.11 = (bf16[128,2048]{1,0:T(8,128)(2,1)S(1)}, bf16[128,2048]{1,0:T(8,128)(2,1)S(1)}, u32[]{:S(2)}, u32[]{:S(2)}) collective-permute-start(bf16[128,2048]{1,0:T(8,128)(2,1)S(1)} %lowered_block.5), channel_id=1, source_target_pairs={{4,1},{5,0},{6,3},{7,2},{8,5},{9,4},{10,7},{11,6},{12,9},{13,8},{1... | collective-permute-start | bytes 1572872 | tf_op jit(solution)/shard_map/ppermute | solution.py:48
  39.1 42.2 %copy-start.3 = (bf16[128,1024]{1,0:T(8,128)(2,1)}, bf16[128,1024]{1,0:T(8,128)(2,1)S(1)}, u32[]{:S(2)}) copy-start(bf16[128,1024]{1,0:T(8,128)(2,1)S(1)} %broadcast_select_fusion.1.cot_ref) | copy-start | bytes 786436
  39.1 42.2 %copy-start.6 = (f32[2048]{0:T(1024)S(1)}, f32[2048]{0:T(1024)}, u32[]{:S(2)}) copy-start(f32[2048]{0:T(1024)} %param.12) | copy-start | bytes 24580
  42.0 39.3 %collective-permute-start.7 = (bf16[128,2048]{1,0:T(8,128)(2,1)}, bf16[128,2048]{1,0:T(8,128)(2,1)}, u32[]{:S(2)}, u32[]{:S(2)}) collective-permute-start(bf16[128,2048]{1,0:T(8,128)(2,1)} %get-tuple-element.47), channel_id=1, source_target_pairs={{0,1},{1,0},{2,3},{3,2},{4,5},{5,4},{6,7},{7,6},{8,9},{9,8},{10,11... | collective-permute-start | bytes 1572872 | tf_op jit(solution)/shard_map/ppermute | solution.py:27
  53.7 57.3 %collective-permute-start.12 = (bf16[128,2048]{1,0:T(8,128)(2,1)}, bf16[128,2048]{1,0:T(8,128)(2,1)}, u32[]{:S(2)}, u32[]{:S(2)}) collective-permute-start(bf16[128,2048]{1,0:T(8,128)(2,1)} %lowered_block.6), channel_id=1, source_target_pairs={{4,2},{5,3},{6,0},{7,1},{8,6},{9,7},{10,4},{11,5},{12,10},{13,11},... | collective-permute-start | bytes 1572872 | tf_op jit(solution)/shard_map/ppermute | solution.py:48
  57.6 53.4 %collective-permute-start.13 = (bf16[128,2048]{1,0:T(8,128)(2,1)}, bf16[128,2048]{1,0:T(8,128)(2,1)}, u32[]{:S(2)}, u32[]{:S(2)}) collective-permute-start(bf16[128,2048]{1,0:T(8,128)(2,1)} %lowered_block.7), channel_id=1, source_target_pairs={{4,3},{5,2},{6,1},{7,0},{8,7},{9,6},{10,5},{11,4},{12,11},{13,10},... | collective-permute-start | bytes 1572872 | tf_op jit(solution)/shard_map/ppermute | solution.py:48
  81.3 29.7 %copy-start.2 = (f32[1024]{0:T(1024)S(1)}, f32[1024]{0:T(1024)}, u32[]{:S(2)}) copy-start(f32[1024]{0:T(1024)} %param.13) | copy-start | bytes 12292
  81.3 0.8 copy-start.5
  88.3 13.7 %collective-permute-start = (f32[8,1024]{1,0:T(8,128)S(1)}, f32[8,1024]{1,0:T(8,128)S(1)}, u32[]{:S(2)}, u32[]{:S(2)}) collective-permute-start(f32[8,1024]{1,0:T(8,128)S(1)} %get-tuple-element.29), channel_id=1, source_target_pairs={{0,1},{1,0},{2,3},{3,2},{4,5},{5,4},{6,7},{7,6},{8,9},{9,8},{10,11... | collective-permute-start | bytes 98312 | tf_op jit(solution)/shard_map/cond/branch_1_fun/ppermute | solution.py:36
  101.9 9.0 %collective-permute-start.1 = (f32[8,1024]{1,0:T(8,128)S(1)}, f32[8,1024]{1,0:T(8,128)S(1)}, u32[]{:S(2)}, u32[]{:S(2)}) collective-permute-start(f32[8,1024]{1,0:T(8,128)S(1)} %add.15), channel_id=1, source_target_pairs={{0,2},{1,3},{2,0},{3,1},{4,6},{5,7},{6,4},{7,5},{8,10},{9,11},{10,... | collective-permute-start | bytes 98312 | tf_op jit(solution)/shard_map/cond/branch_1_fun/ppermute | solution.py:36
